TPU v7x, 128 devices: a whole 4x4x4 slice. The times are simulated.
128 devices in a mesh: group: 8 (over x, y_hi), replica: 16 (over z, y_lo, core).
Axes of the slice: x: 4, y: 4 (y_hi: 2, y_lo: 2; y = y_hi * 2 + y_lo), z: 4, core: 2. Of those that a mesh axis runs over, the one named last changes fastest.
Arguments:
- tokens: bfloat16 [16, 1024, 1152], P('replica', 'group'), may hold values from -6 to 6
- positions: int32 [16, 1024], P('replica', 'group'), may hold values from 0 to 1023, as said below
- cotangent: bfloat16 [16, 1024, 1152], P('replica', 'group'), may hold values from -6 to 6
- gain_attn: float32 [1152], replicated, may hold values from 0.25 to 1.75
- gain_query: float32 [256], replicated, may hold values from 0.25 to 1.75
- gain_key: float32 [256], replicated, may hold values from 0.25 to 1.75
- gain_post_attn: float32 [1152], replicated, may hold values from 0.25 to 1.75
- gain_ffn: float32 [1152], replicated, may hold values from 0.25 to 1.75
- gain_post_ffn: float32 [1152], replicated, may hold values from 0.25 to 1.75
- w_query: bfloat16 [1152, 1024], P('group'), may hold values from -0.1875 to 0.1875
- w_key: bfloat16 [1152, 256], P('group'), may hold values from -0.1875 to 0.1875
- w_value: bfloat16 [1152, 256], P('group'), may hold values from -0.1875 to 0.1875
- w_out: bfloat16 [1152, 1024], P('group'), may hold values from -0.1875 to 0.1875
- w_gate: bfloat16 [1152, 6912], P('group'), may hold values from -0.1875 to 0.1875
- w_up: bfloat16 [1152, 6912], P('group'), may hold values from -0.1875 to 0.1875
- w_down: bfloat16 [1152, 6912], P('group'), may hold values from -0.078125 to 0.078125
Outputs:
- mixed_out: bfloat16 [16, 1024, 1152], P('replica', 'group')
- grad_tokens: float32 [16, 1024, 1152], P('replica', 'group')
- grad_gain_attn: float32 [1152], replicated
- grad_gain_query: float32 [256], replicated
- grad_gain_key: float32 [256], replicated
- grad_gain_post_attn: float32 [1152], replicated
- grad_gain_ffn: float32 [1152], replicated
- grad_gain_post_ffn: float32 [1152], replicated
- grad_query: float32 [1152, 1024], P('group')
- grad_key: float32 [1152, 256], P('group')
- grad_value: float32 [1152, 256], P('group')
- grad_out: float32 [1152, 1024], P('group')
- grad_gate: float32 [1152, 6912], P('group')
- grad_up: float32 [1152, 6912], P('group')
- grad_down: float32 [1152, 6912], P('group')
Inputs may be any that keep to these rules, and one draw needn't show every extreme that they name: Within a sequence, positions rise by one from token to token inside a document and are 0 at a document's first token; the first document starts at the sequence's first token. In each block of 1 sequence one document leaves fewer than 128 tokens of its sequence before it and after it; one sequence of the first block is a single document.
All inputs are finite; a program needn't handle non-finite values.
Results may differ from a plain program's by a relative error of at most 0.025.
Values may be sent and summed in bfloat16 or wider, within the bound.
No kernel may reach another device: no remote copies, remote signals or barrier semaphores. Data moves between devices by JAX's collectives and lax.ppermute only.
A program may use at most 320 MiB of HBM per device.

v0:
```python
import jax
import jax.numpy as jnp
from jax import lax
from jax.sharding import PartitionSpec as P

HEADS = 4
WINDOW = 512


EPSILON = 1e-06
ROPE_BASE = 10000.0
MASKED = -1e30
CONTRACT_COLS = (((1,), (1,)), ((), ()))
CONTRACT_ROWS = (((0,), (0,)), ((), ()))


def from_behind(block, axis, distance):
    devices = range(lax.axis_size(axis))
    route = [(i - distance, i) for i in devices if i - distance in devices]
    return lax.ppermute(block, axis, route)


def norm_rows(entries, gain_row):
    return (
        entries
        * lax.rsqrt(jnp.mean(entries * entries, axis=-1, keepdims=True) + EPSILON)
        * gain_row
    )


def turn_tables(position_rows, head_width):
    half_width = head_width // 2
    frequency = ROPE_BASE ** (-2.0 * jnp.arange(half_width, dtype=jnp.float32) / head_width)
    angles = position_rows.astype(jnp.float32)[..., None] * frequency
    return (jnp.cos(angles), jnp.sin(angles))


def rotate(entries, cosine_table, sine_table):
    half_width = entries.shape[-1] // 2
    leading = entries[..., :half_width]
    trailing = entries[..., half_width:]
    return jnp.concatenate(
        [
            leading * cosine_table - trailing * sine_table,
            trailing * cosine_table + leading * sine_table,
        ],
        axis=-1,
    )


def query_piece(raw_proj, gain_row, cosine_table, sine_table):
    head_width = gain_row.shape[0]
    shaped = raw_proj.reshape(cosine_table.shape[0], cosine_table.shape[1], -1, head_width)
    turned = rotate(
        norm_rows(shaped, gain_row), cosine_table[:, :, None, :], sine_table[:, :, None, :]
    )
    return jnp.transpose(turned, (0, 2, 1, 3)) * head_width ** (-0.5)


def key_piece(raw_proj, gain_row, cosine_table, sine_table):
    shaped = raw_proj.reshape(cosine_table.shape[0], cosine_table.shape[1], gain_row.shape[0])
    return rotate(norm_rows(shaped, gain_row), cosine_table, sine_table)


def gelu_product(gate_proj, up_proj):
    return jax.nn.gelu(gate_proj, approximate=True) * up_proj


def masked_scores(queries, key_rows, allowed):
    plain = jnp.einsum("shqd,skd->shqk", queries, key_rows, preferred_element_type=jnp.float32)
    return jnp.where(allowed, plain, MASKED)


def transposed_product(left_side, right_side):
    return lax.dot_general(left_side, right_side, CONTRACT_ROWS, preferred_element_type=jnp.float32)


def product_by_rows(left_side, right_side):
    return lax.dot_general(left_side, right_side, CONTRACT_COLS, preferred_element_type=jnp.float32)


def replica_total(shards):
    return (
        lax.psum(shards[0].astype(jnp.bfloat16), "replica").astype(jnp.float32),
        lax.psum(shards[1].astype(jnp.bfloat16), "replica").astype(jnp.float32),
    )


def local(
    tokens,
    positions,
    cotangent,
    gain_attn,
    gain_query,
    gain_key,
    gain_post_attn,
    gain_ffn,
    gain_post_ffn,
    w_query,
    w_key,
    w_value,
    w_out,
    w_gate,
    w_up,
    w_down,
):
    seq_count, tok_rows, model_width = tokens.shape
    all_rows = seq_count * tok_rows
    head_width = gain_query.shape[0]
    query_cols = w_query.shape[1]
    unit_count = w_gate.shape[1]
    reach_back = min(-(-(WINDOW - 1) // tok_rows), lax.axis_size("group") - 1)
    cosine_table, sine_table = turn_tables(positions, head_width)
    inputs = tokens.astype(jnp.float32).reshape(all_rows, model_width)
    normed_full, norm_attn_back = jax.vjp(norm_rows, inputs, gain_attn)
    normed = normed_full.astype(jnp.bfloat16)
    pieces = (
        lax.all_gather(w_query, "group", axis=0, tiled=True),
        lax.all_gather(w_key, "group", axis=0, tiled=True),
        lax.all_gather(w_value, "group", axis=0, tiled=True),
    )
    left_cols = normed
    query_raw, key_raw, value_raw = tuple(
        (jnp.dot(left_cols, matrix, preferred_element_type=jnp.float32) for matrix in pieces)
    )

    def query_local(raw_proj, gain_row):
        return query_piece(raw_proj, gain_row, cosine_table, sine_table)

    def key_local(raw_proj, gain_row):
        return key_piece(raw_proj, gain_row, cosine_table, sine_table)

    queries_full, query_back = jax.vjp(query_local, query_raw, gain_query)
    keys_full, key_back = jax.vjp(key_local, key_raw, gain_key)
    queries = queries_full.astype(jnp.bfloat16)
    local_pairs = jnp.concatenate(
        [keys_full, value_raw.reshape(seq_count, tok_rows, head_width)], axis=-1
    ).astype(jnp.bfloat16)
    collected = [local_pairs]
    for distance in range(1, reach_back + 1):
        collected.insert(0, from_behind(local_pairs, "group", distance))
    pair_rows = jnp.concatenate(collected, axis=1)
    key_rows = pair_rows[..., :head_width]
    value_rows = pair_rows[..., head_width:]
    group_index = lax.axis_index("group")
    query_index = group_index * tok_rows + jnp.arange(tok_rows, dtype=jnp.int32)
    key_index = (group_index - reach_back) * tok_rows + jnp.arange(
        (reach_back + 1) * tok_rows, dtype=jnp.int32
    )
    offsets = query_index[:, None] - key_index[None, :]
    doc_start = query_index[None, :] - positions
    allowed = ((offsets >= 0) & (offsets < WINDOW))[None, :, :] & (
        key_index[None, None, :] >= doc_start[:, :, None]
    )
    allowed = allowed[:, None, :, :]
    scores = masked_scores(queries, key_rows, allowed)
    highest = jnp.max(scores, axis=-1, keepdims=True)
    exp_scores = jnp.exp(scores - highest)
    sum_scores = jnp.sum(exp_scores, axis=-1, keepdims=True)
    log_total = highest + jnp.log(sum_scores)
    weights = (exp_scores / sum_scores).astype(jnp.bfloat16)
    mixed_heads = jnp.einsum(
        "shqk,skd->sqhd", weights, value_rows, preferred_element_type=jnp.float32
    )
    attended = mixed_heads.reshape(all_rows, query_cols).astype(jnp.bfloat16)
    attn_branch = product_by_rows(attended, lax.all_gather(w_out, "group", axis=0, tiled=True))
    attn_normed, norm_post_attn_back = jax.vjp(norm_rows, attn_branch, gain_post_attn)
    middle = inputs + attn_normed
    ffn_in_full, norm_ffn_back = jax.vjp(norm_rows, middle, gain_ffn)
    normed_ffn = ffn_in_full.astype(jnp.bfloat16)
    pieces = (
        lax.all_gather(w_gate, "group", axis=0, tiled=True),
        lax.all_gather(w_up, "group", axis=0, tiled=True),
    )
    left_cols = normed_ffn
    gate_proj = jnp.dot(left_cols, pieces[0], preferred_element_type=jnp.float32)
    up_proj = jnp.dot(left_cols, pieces[1], preferred_element_type=jnp.float32)
    hidden_full, gelu_back = jax.vjp(gelu_product, gate_proj, up_proj)
    hidden = hidden_full.astype(jnp.bfloat16)
    ffn_branch = product_by_rows(hidden, lax.all_gather(w_down, "group", axis=0, tiled=True))
    ffn_normed, norm_post_ffn_back = jax.vjp(norm_rows, ffn_branch, gain_post_ffn)
    outputs = (middle + ffn_normed).astype(jnp.bfloat16).reshape(seq_count, tok_rows, model_width)
    upstream = cotangent.astype(jnp.float32).reshape(all_rows, model_width)
    grad_ffn_branch, grad_post_ffn = norm_post_ffn_back(upstream)
    grad_ffn_branch = grad_ffn_branch.astype(jnp.bfloat16)
    grad_hidden = jnp.dot(
        grad_ffn_branch,
        lax.all_gather(w_down, "group", axis=0, tiled=True),
        preferred_element_type=jnp.float32,
    )
    grad_gate_full, grad_up_full = gelu_back(grad_hidden)
    grad_units = jnp.concatenate([grad_gate_full, grad_up_full], axis=1).astype(jnp.bfloat16)
    grad_gate_part = grad_units[:, :unit_count]
    grad_up_part = grad_units[:, unit_count:]
    pieces = (
        lax.all_gather(w_gate, "group", axis=0, tiled=True),
        lax.all_gather(w_up, "group", axis=0, tiled=True),
    )
    contribution = product_by_rows(grad_gate_part, pieces[0]) + product_by_rows(
        grad_up_part, pieces[1]
    )
    grad_normed_ffn = contribution
    ffn_grads = lax.psum_scatter(
        jnp.concatenate(
            [
                transposed_product(normed_ffn, grad_units),
                transposed_product(grad_ffn_branch, hidden),
            ],
            axis=1,
        ).astype(jnp.bfloat16),
        "group",
        scatter_dimension=0,
        tiled=True,
    ).astype(jnp.float32)
    grad_middle_part, grad_gain_ffn = norm_ffn_back(grad_normed_ffn)
    grad_middle = upstream + grad_middle_part
    grad_attn_branch, grad_post_attn = norm_post_attn_back(grad_middle)
    grad_attn_branch = grad_attn_branch.astype(jnp.bfloat16)
    grad_attended = jnp.dot(
        grad_attn_branch,
        lax.all_gather(w_out, "group", axis=0, tiled=True),
        preferred_element_type=jnp.float32,
    )
    grad_heads = grad_attended.astype(jnp.bfloat16).reshape(seq_count, tok_rows, HEADS, head_width)
    scores = masked_scores(queries, key_rows, allowed)
    probabilities = jnp.exp(scores - log_total)
    grad_probs = jnp.einsum(
        "sqhd,skd->shqk", grad_heads, value_rows, preferred_element_type=jnp.float32
    )
    centre = jnp.sum(probabilities * grad_probs, axis=-1, keepdims=True)
    grad_scores = (probabilities * (grad_probs - centre)).astype(jnp.bfloat16)
    grad_queries = jnp.einsum(
        "shqk,skd->shqd", grad_scores, key_rows, preferred_element_type=jnp.float32
    )
    grad_key_rows = jnp.einsum(
        "shqk,shqd->skd", grad_scores, queries, preferred_element_type=jnp.float32
    )
    grad_value_rows = jnp.einsum(
        "shqk,sqhd->skd",
        probabilities.astype(jnp.bfloat16),
        grad_heads,
        preferred_element_type=jnp.float32,
    )
    grad_pairs = jnp.concatenate([grad_key_rows, grad_value_rows], axis=-1)
    own_pairs = grad_pairs[:, reach_back * tok_rows :]
    for distance in range(1, reach_back + 1):
        lower_block = reach_back - distance
        sent_block = grad_pairs[:, lower_block * tok_rows : (lower_block + 1) * tok_rows]
        own_pairs = own_pairs + from_behind(
            sent_block.astype(jnp.bfloat16), "group", -distance
        ).astype(sent_block.dtype)
    grad_key_raw, grad_gain_key = key_back(own_pairs[..., :head_width])
    grad_query_raw, grad_gain_query = query_back(grad_queries)
    grad_value_raw = own_pairs[..., head_width:].reshape(all_rows, head_width)
    grad_projected = jnp.concatenate([grad_query_raw, grad_key_raw, grad_value_raw], axis=1).astype(
        jnp.bfloat16
    )
    grad_query_part = grad_projected[:, :query_cols]
    grad_key_part = grad_projected[:, query_cols : query_cols + head_width]
    grad_value_part = grad_projected[:, query_cols + head_width :]
    pieces = (
        lax.all_gather(w_query, "group", axis=0, tiled=True),
        lax.all_gather(w_key, "group", axis=0, tiled=True),
        lax.all_gather(w_value, "group", axis=0, tiled=True),
    )
    contribution = (
        product_by_rows(grad_query_part, pieces[0])
        + product_by_rows(grad_key_part, pieces[1])
        + product_by_rows(grad_value_part, pieces[2])
    )
    attn_grads = lax.psum_scatter(
        jnp.concatenate(
            [
                transposed_product(normed, grad_projected),
                transposed_product(grad_attn_branch, attended),
            ],
            axis=1,
        ).astype(jnp.bfloat16),
        "group",
        scatter_dimension=0,
        tiled=True,
    ).astype(jnp.float32)
    ffn_grads, attn_grads = replica_total((ffn_grads, attn_grads))
    grad_inputs_part, grad_gain_attn = norm_attn_back(contribution)
    grad_tokens = (grad_middle + grad_inputs_part).reshape(seq_count, tok_rows, model_width)
    gain_sums = lax.psum(
        (
            grad_gain_attn,
            grad_gain_query,
            grad_gain_key,
            grad_post_attn,
            grad_gain_ffn,
            grad_post_ffn,
        ),
        ("group", "replica"),
    )
    key_end = query_cols + head_width
    value_end = key_end + head_width
    return (
        outputs,
        grad_tokens,
        gain_sums[0],
        gain_sums[1],
        gain_sums[2],
        gain_sums[3],
        gain_sums[4],
        gain_sums[5],
        attn_grads[:, :query_cols],
        attn_grads[:, query_cols:key_end],
        attn_grads[:, key_end:value_end],
        attn_grads[:, value_end:],
        ffn_grads[:, :unit_count],
        ffn_grads[:, unit_count : 2 * unit_count],
        ffn_grads[:, 2 * unit_count :],
    )


def solution(mesh):
    placed = (
        P("replica", "group", None),
        P("replica", "group"),
        P("replica", "group", None),
        P(),
        P(),
        P(),
        P(),
        P(),
        P(),
        P("group", None),
        P("group", None),
        P("group", None),
        P("group", None),
        P("group", None),
        P("group", None),
        P("group", None),
    )
    return jax.shard_map(
        local,
        mesh=mesh,
        in_specs=placed,
        out_specs=(
            P("replica", "group", None),
            P("replica", "group", None),
            P(),
            P(),
            P(),
            P(),
            P(),
            P(),
            P("group", None),
            P("group", None),
            P("group", None),
            P("group", None),
            P("group", None),
            P("group", None),
            P("group", None),
        ),
        check_vma=False,
    )
```

profile of v0, /device:TPU:1, one launch (start us, length us, event | category | flops | bytes accessed | tf_op | source)
XLA Modules:
  0.0 1520.0 jit_solution(8957635959175877151)
XLA Ops:
  10.9 30.6 %all_gather.29 = bf16[1152,256]{1,0:T(8,128)(2,1)S(1)} all-gather(bf16[144,256]{1,0:T(8,128)(2,1)S(1)} %copy-done.45), channel_id=1, replica_groups=mesh['group'=8,'replica'=16] {'group'}, dimensions={0}, use_global_device_ids=true | all-gather | bytes 663552 | tf_op jit(solution)/shard_map/all_gather | solution.py:120
  42.7 31.3 %all_gather.28 = bf16[1152,256]{1,0:T(8,128)(2,1)S(1)} all-gather(bf16[144,256]{1,0:T(8,128)(2,1)S(1)} %copy-done.46), channel_id=1, replica_groups=mesh['group'=8,'replica'=16] {'group'}, dimensions={0}, use_global_device_ids=true | all-gather | bytes 663552 | tf_op jit(solution)/shard_map/all_gather | solution.py:119
  75.8 3.4 collective-permute-start.3
  79.1 1.9 collective-permute-start.2
  81.1 4.3 collective-permute-start.1
  85.4 3.0 collective-permute-start
  89.0 1.4 collective-permute-done
  90.5 2.5 fusion.84
  95.7 42.5 %all-gather.8.cloned.1.call-done = bf16[1152,1024]{1,0:T(8,128)(2,1)} async-done(((bf16[144,1024]{1,0:T(8,128)(2,1)}), bf16[1152,1024]{1,0:T(8,128)(2,1)}) %all-gather.8.cloned.1.call-update) | async-done | bytes 2359312 | tf_op jit(solution)/shard_map/all_gather | solution.py:166
  138.2 2.6 multiply_reduce_fusion.6
  142.3 175.7 %all-gather.10.cloned.1.call-done = bf16[1152,6912]{1,0:T(8,128)(2,1)} async-done(((bf16[144,6912]{1,0:T(8,128)(2,1)}), bf16[1152,6912]{1,0:T(8,128)(2,1)}) %all-gather.10.cloned.1.call-update) | async-done | bytes 15925264 | tf_op jit(solution)/shard_map/all_gather | solution.py:172
  318.0 9.8 fusion.95
  327.8 168.4 %all-gather.12.cloned.1.call-done = bf16[1152,6912]{1,0:T(8,128)(2,1)} async-done(((bf16[144,6912]{1,0:T(8,128)(2,1)}), bf16[1152,6912]{1,0:T(8,128)(2,1)}) %all-gather.12.cloned.1.call-update) | async-done | bytes 15925264 | tf_op jit(solution)/shard_map/all_gather | solution.py:173
  496.2 11.4 multiply_convert_fusion.1
  507.6 166.8 %all-gather.14.cloned.1.call-done = bf16[1152,6912]{1,0:T(8,128)(2,1)} async-done(((bf16[144,6912]{1,0:T(8,128)(2,1)}), bf16[1152,6912]{1,0:T(8,128)(2,1)}) %all-gather.14.cloned.1.call-update) | async-done | bytes 15925264 | tf_op jit(solution)/shard_map/all_gather | solution.py:180
  674.5 10.7 multiply_reduce_fusion.4
  685.4 1.0 fusion.27
  686.4 14.1 multiply_convert_fusion
  700.5 11.9 fusion.96
  712.4 12.1 multiply_reduce_fusion
  724.5 2.3 multiply_reduce_fusion.1
  728.3 1.2 convolution_convert_fusion.4
  729.6 1.8 copy.114
  731.4 1.5 convolution_bitcast_fusion.1
  732.9 1.8 fusion.11
  736.0 2.2 convolution_convert_fusion.3
  740.0 1.3 collective-permute-start.4
  741.3 1.3 collective-permute-start.7
  742.6 1.3 collective-permute-start.6
  743.9 1.5 collective-permute-start.5
  746.3 1.1 copy.97
  747.4 1.6 collective-permute-done.7
  749.0 2.0 collective-permute-done.6
  751.0 1.2 fusion.49
  755.6 1.2 convolution_convert_fusion.2
  757.3 2.9 pad_maximum_fusion.1
  761.2 7.8 convolution_convert_fusion.1
  768.9 15.4 %convolution_convert_fusion = bf16[1152,13824]{1,0:T(8,128)(2,1)} fusion(bf16[128,1152]{1,0:T(8,128)(2,1)S(1)} %copy-done.15, bf16[128,6912]{1,0:T(8,128)(2,1)S(1)} %copy-done.10, bf16[128,6912]{1,0:T(8,128)(2,1)} %get-tuple-element.39), kind=kOutput, calls=%fused_computation | convolution fusion | flops 4099866624 | bytes 35684352 | tf_op jit(solution)/shard_map/dot_general | solution.py:75
  784.4 32.8 %pad_maximum_fusion = bf16[1152,20736]{1,0:T(8,128)(2,1)} fusion(bf16[1152,6912]{1,0:T(8,128)(2,1)} %convolution_convert_fusion.1, bf16[1152,13824]{1,0:T(8,128)(2,1)} %convolution_convert_fusion), kind=kLoop, calls=%fused_computation.1 | loop fusion | flops 95551488 | bytes 95551488 | tf_op jit(solution)/shard_map/concatenate | solution.py:204
  817.3 44.2 %reduce-scatter.3.cloned.1.call-done = bf16[144,2560]{1,0:T(8,128)(2,1)} async-done(((bf16[1152,2560]{1,0:T(8,128)(2,1)}), bf16[144,2560]{1,0:T(8,128)(2,1)}) %reduce-scatter.3.cloned.1.call-update) | async-done | bytes 737296 | tf_op jit(solution)/shard_map/reduce_scatter | solution.py:271
  861.5 472.4 %reduce-scatter.5.cloned.1.call-done = bf16[144,20736]{1,0:T(8,128)(2,1)} async-done(((bf16[1152,20736]{1,0:T(8,128)(2,1)}), bf16[144,20736]{1,0:T(8,128)(2,1)}) %reduce-scatter.5.cloned.1.call-update) | async-done | bytes 5971984 | tf_op jit(solution)/shard_map/reduce_scatter | solution.py:203
  1334.0 2.0 fusion.97
  1336.8 68.6 %all-reduce.4 = (f32[1152]{0:T(1024)}, f32[256]{0:T(256)}, f32[256]{0:T(256)}, f32[1152]{0:T(1024)}, f32[1152]{0:T(1024)}, /*index=5*/f32[1152]{0:T(1024)}) all-reduce(f32[1152]{0:T(1024)S(1)} %get-tuple-element.23, f32[256]{0:T(256)S(1)} %copy-done.65, ...), channel_id=1, replica_groups=mesh['group'=8,'replica'=16] {'group','replica'}, use_global_device_ids=true, to_apply=%region_16.17 | all-reduce | flops 5120 | bytes 40960 | tf_op jit(solution)/shard_map/psum | solution.py:286
  1405.4 1.0 fusion.30
  1406.4 95.1 %all-reduce.8.cloned.1.call-done = (bf16[144,2560]{1,0:T(8,128)(2,1)}, bf16[144,20736]{1,0:T(8,128)(2,1)}) async-done(((bf16[144,2560]{1,0:T(8,128)(2,1)}, bf16[144,20736]{1,0:T(8,128)(2,1)}), (bf16[144,2560]{1,0:T(8,128)(2,1)}, bf16[144,20736]{1,0:T(8,128)(2,1)})) %all-reduce.8.cloned.1.call-update) | async-done | bytes 6709264 | tf_op jit(solution)/shard_map/psum | solution.py:85
  1501.5 1.7 fusion.91
  1503.2 2.2 fusion.90
  1505.4 7.6 fusion.89
  (228 shorter events, 22.2 us)
Async XLA Ops:
  7.2 83.3 %all-gather.6.cloned.1.call-start = ((), (), s32[]{:S(2)}) async-start(), calls=%async_computation.2 | async-start | bytes 2654208 | tf_op jit(solution)/shard_map/all_gather | solution.py:118
  7.9 130.2 %all-gather.8.cloned.1.call-start = ((), (), s32[]{:S(2)}) async-start(), calls=%async_computation.3 | async-start | bytes 2654208 | tf_op jit(solution)/shard_map/all_gather | solution.py:166
  8.7 33.7 %copy-start.42 = (f32[1152]{0:T(1024)S(1)}, f32[1152]{0:T(1024)}, u32[]{:S(2)}) copy-start(f32[1152]{0:T(1024)} %param.19) | copy-start | bytes 13828
  8.7 34.0 %copy-start.46 = (bf16[144,256]{1,0:T(8,128)(2,1)S(1)}, bf16[144,256]{1,0:T(8,128)(2,1)}, u32[]{:S(2)}) copy-start(bf16[144,256]{1,0:T(8,128)(2,1)} %param.26) | copy-start | bytes 221188
  8.7 309.3 %all-gather.10.cloned.1.call-start = ((), (), s32[]{:S(2)}) async-start(), calls=%async_computation.4 | async-start | bytes 17915904 | tf_op jit(solution)/shard_map/all_gather | solution.py:172
  9.4 65.7 %copy-start.70 = (s32[1,128]{1,0:T(1,128)S(1)}, s32[1,128]{1,0:T(1,128)}, u32[]{:S(2)}) copy-start(s32[1,128]{1,0:T(1,128)} %param.17) | copy-start | bytes 1540
  9.4 65.8 %copy-start.51 = (f32[256]{0:T(256)S(1)}, f32[256]{0:T(256)}, u32[]{:S(2)}) copy-start(f32[256]{0:T(256)} %param.21) | copy-start | bytes 3076
  9.5 486.8 %all-gather.12.cloned.1.call-start = ((), (), s32[]{:S(2)}) async-start(), calls=%async_computation.5 | async-start | bytes 17915904 | tf_op jit(solution)/shard_map/all_gather | solution.py:173
  10.0 664.4 %all-gather.14.cloned.1.call-start = ((), (), s32[]{:S(2)}) async-start(), calls=%async_computation.6 | async-start | bytes 17915904 | tf_op jit(solution)/shard_map/all_gather | solution.py:180
  10.6 850.8 %reduce-scatter.3.cloned.1.call-start = ((), (), s32[]{:S(2)}) async-start(), calls=%async_computation.7 | async-start | bytes 6635520 | tf_op jit(solution)/shard_map/reduce_scatter | solution.py:271
  10.7 79.8 %copy-start.62 = (f32[128]{0:T(128)}, f32[128]{0:T(128)S(1)}, u32[]{:S(2)}) copy-start(f32[128]{0:T(128)S(1)} %multiply_power_fusion) | copy-start | bytes 1540
  10.9 64.3 %copy-start.68 = (f32[128]{0:T(128)}, f32[128]{0:T(128)S(1)}, u32[]{:S(2)}) copy-start(f32[128]{0:T(128)S(1)} %fusion.32) | copy-start | bytes 1540
  10.9 82.2 %copy-start.57 = (f32[128]{0:T(128)}, f32[128]{0:T(128)S(1)}, u32[]{:S(2)}) copy-start(f32[128]{0:T(128)S(1)} %fusion.72) | copy-start | bytes 1540
  75.2 18.1 %copy-start.55 = (f32[128]{0:T(128)}, f32[128]{0:T(128)S(1)}, u32[]{:S(2)}) copy-start(f32[128]{0:T(128)S(1)} %get-tuple-element.63) | copy-start | bytes 1540
  75.2 18.4 %copy-start.53 = (f32[256]{0:T(256)S(1)}, f32[256]{0:T(256)}, u32[]{:S(2)}) copy-start(f32[256]{0:T(256)} %param.20) | copy-start | bytes 3076
  75.8 14.7 collective-permute-start.3
  79.1 11.3 collective-permute-start.2
  81.1 9.3 collective-permute-start.1
  85.4 5.0 collective-permute-start
  95.0 45.8 %copy-start.44 = (f32[1152]{0:T(1024)S(1)}, f32[1152]{0:T(1024)}, u32[]{:S(2)}) copy-start(f32[1152]{0:T(1024)} %param.22) | copy-start | bytes 13828
  95.7 45.7 %copy-start.32 = (bf16[256,4,128]{2,0,1:T(8,128)(2,1)}, bf16[256,4,128]{2,0,1:T(8,128)(2,1)S(1)}, u32[]{:S(2)}) copy-start(bf16[256,4,128]{2,0,1:T(8,128)(2,1)S(1)} %convolution_convert_fusion.5) | copy-start | bytes 786436
  95.7 46.4 %copy-start.43 = (f32[1152]{0:T(1024)S(1)}, f32[1152]{0:T(1024)}, u32[]{:S(2)}) copy-start(f32[1152]{0:T(1024)} %param.23) | copy-start | bytes 13828
  140.8 187.0 %copy-start.8 = (f32[128,1152]{1,0:T(8,128)}, f32[128,1152]{1,0:T(8,128)S(1)}, u32[]{:S(2)}) copy-start(f32[128,1152]{1,0:T(8,128)S(1)} %get-tuple-element.70) | copy-start | bytes 1769476
  141.3 186.5 %copy-start.66 = (f32[128]{0:T(128)}, f32[128]{0:T(128)S(1)}, u32[]{:S(2)}) copy-start(f32[128]{0:T(128)S(1)} %get-tuple-element.36) | copy-start | bytes 1540
  141.4 186.4 %copy-start.63 = (f32[128]{0:T(128)}, f32[128]{0:T(128)S(1)}, u32[]{:S(2)}) copy-start(f32[128]{0:T(128)S(1)} %fusion.75) | copy-start | bytes 1540
  142.3 185.5 %copy-start.14 = (bf16[128,1152]{1,0:T(8,128)(2,1)}, bf16[128,1152]{1,0:T(8,128)(2,1)S(1)}, u32[]{:S(2)}) copy-start(bf16[128,1152]{1,0:T(8,128)(2,1)S(1)} %multiply_convert_fusion.2) | copy-start | bytes 884740
  674.4 10.7 copy-start.16
  674.4 10.7 copy-start.47
  674.5 11.0 copy-start.1
  686.4 14.1 copy-start.26
  700.5 11.9 copy-start.64
  712.4 12.1 copy-start.67
  712.4 12.1 copy-start.9
  712.4 12.1 copy-start.60
  712.4 14.4 copy-start.72
  739.1 13.1 copy-start.56
  739.1 14.2 copy-start.52
  739.2 16.4 %copy-start.58 = (f32[128]{0:T(128)S(1)}, f32[128]{0:T(128)}, u32[]{:S(2)}) copy-start(f32[128]{0:T(128)} %copy-done.57) | copy-start | bytes 1540
  740.0 7.4 collective-permute-start.4
  741.3 7.7 collective-permute-start.7
  742.6 8.4 collective-permute-start.6
  743.9 7.1 collective-permute-start.5
  747.4 9.5 copy-start.21
  760.3 573.6 %reduce-scatter.5.cloned.1.call-start = ((), (), s32[]{:S(2)}) async-start(), calls=%async_computation.8 | async-start | bytes 53747712 | tf_op jit(solution)/shard_map/reduce_scatter | solution.py:203
  817.2 516.7 %copy-start.5 = (bf16[1152,1024]{1,0:T(8,128)(2,1)S(1)}, bf16[1152,1024]{1,0:T(8,128)(2,1)}, u32[]{:S(2)}) copy-start(bf16[1152,1024]{1,0:T(8,128)(2,1)} %all-gather.6.cloned.1.call-done) | copy-start | bytes 7077892
  817.2 684.3 %all-reduce.8.cloned.1.call-start = ((), (), s32[]{:S(2)}) async-start(), calls=%async_computation.9 | async-start | bytes 13418496 | tf_op jit(solution)/shard_map/psum | solution.py:85
  1334.0 71.5 %copy-start.69 = (f32[128]{0:T(128)S(1)}, f32[128]{0:T(128)}, u32[]{:S(2)}) copy-start(f32[128]{0:T(128)} %copy-done.68) | copy-start | bytes 1540
  1334.0 71.5 %copy-start.13 = (f32[128,1152]{1,0:T(8,128)S(1)}, f32[128,1152]{1,0:T(8,128)}, u32[]{:S(2)}) copy-start(f32[128,1152]{1,0:T(8,128)} %copy-done.12) | copy-start | bytes 1769476
  (42 other events, 116.1 us)
Sparse Core Ops, SparseCore 0:
  10.3 68.3 all-gather.5
  81.0 57.1 all-gather.7
  140.5 177.4 all-gather.9
  320.2 175.9 all-gather.11
  498.4 175.9 all-gather.13
  760.4 101.0 reduce-scatter.2
  866.0 467.8 reduce-scatter.4
  1336.7 164.8 all-reduce.7
where the time goes:
time: 1540 us; the launch traced here: 1520 us
  waiting for transfers between devices  1170 us (76%)
  blocking collectives  131 us (9%)
  matrix products  112 us (7%)
  other arithmetic  49.1 us (3%)
  local copies, waits for them, and re-layouts  21.6 us (1%)
  starting transfers between devices  18.3 us (1%)
  between operations  15.6 us (1%)
    reduce_scatter x1, waiting for transfers between devices, local(): lax.psum_scatter(jnp.concatenate([transposed_product(normed_ffn, grad_uni...  472 us
    all_gather x1, waiting for transfers between devices, local(): lax.all_gather(w_gate, 'group', axis=0, tiled=True)  176 us
    all_gather x1, waiting for transfers between devices, local(): lax.all_gather(w_up, 'group', axis=0, tiled=True)  168 us
    all_gather x1, waiting for transfers between devices, local(): lax.all_gather(w_down, 'group', axis=0, tiled=True)  167 us
    psum x1, waiting for transfers between devices, replica_total(): lax.psum(shards[1].astype(jnp.bfloat16), 'replica').astype(jnp.float32)  95.1 us
    psum x1, blocking collectives, local(): lax.psum((grad_gain_attn, grad_gain_query, grad_gain_key, grad_post_attn,...  68.6 us
    reduce_scatter x1, waiting for transfers between devices, local(): lax.psum_scatter(jnp.concatenate([transposed_product(normed, grad_project...  44.2 us
    all_gather x1, waiting for transfers between devices, local(): lax.all_gather(w_out, 'group', axis=0, tiled=True)  42.5 us
  transfers between devices with their start and end apart: 16, of which 10 were waited for; matrix products, arithmetic and copies ran while one was open for 6% of the time, Pallas kernels for 0%

commit v1 on v0

v1 whole, which is shorter than its diff:
```python
import jax
import jax.numpy as jnp
from jax import lax
from jax.experimental import pallas as pl
from jax.experimental.pallas import tpu as pltpu
from jax.sharding import Mesh
from jax.sharding import PartitionSpec as P

HEADS = 4
WINDOW = 512


EPSILON = 1e-06
ROPE_BASE = 10000.0
MASKED = -1e30
CONTRACT_COLS = (((1,), (1,)), ((), ()))
CONTRACT_ROWS = (((0,), (0,)), ((), ()))


GROUP = ("x", "yh")
REPLICA = ("z", "yl", "core")
SHIFTS = ((1, 0), (3, 0), (0, 1), (1, 1), (3, 1), (2, 0), (2, 1))
Z_STEPS = (1, 3, 2)
LANES = 128
UNIT_TILES = 7


def from_behind(block, distance):
    devices = range(8)
    route = [(i - distance, i) for i in devices if i - distance in devices]
    return lax.ppermute(block, GROUP, route)


def shifted(block, step):
    route = [(a * 2 + b, (a + step[0]) % 4 * 2 + (b ^ step[1])) for a in range(4) for b in range(2)]
    return lax.ppermute(block, GROUP, route)


def turned(block, axis, step, size):
    return lax.ppermute(block, axis, [(i, (i + step) % size) for i in range(size)])


def swapped(block, axis):
    return turned(block, axis, 1, 2)


def pick(stack, index):
    return lax.dynamic_index_in_dim(stack, index, 0, keepdims=False)


def place(stack, block, index):
    return lax.dynamic_update_index_in_dim(stack, block, index, 0)


def group_index(step=(0, 0), sign=1):
    along_x = lax.rem(lax.axis_index("x") + 4 + sign * step[0], 4)
    return along_x * 2 + (lax.axis_index("yh") ^ step[1])


def gather_rows(shard):
    stack = place(jnp.zeros((8,) + shard.shape, shard.dtype), shard, group_index())
    for step in SHIFTS:
        stack = place(stack, shifted(shard, step), group_index(step, -1))
    return stack.reshape((-1,) + shard.shape[1:])


def by_core(first, second):
    held = jnp.where(lax.axis_index("core") == 0, first, second)
    return held


def core_pair(held):
    other = swapped(held, "core")
    is_first = lax.axis_index("core") == 0
    return jnp.where(is_first, held, other), jnp.where(is_first, other, held)


def gather_tokens(rows):
    return jnp.concatenate([rows] + [shifted(rows, step) for step in SHIFTS], axis=0)


def scatter_tokens(partial):
    rows = partial.shape[0] // 8
    total = partial[:rows]
    for i, step in enumerate(SHIFTS):
        back = ((4 - step[0]) % 4, step[1])
        block = partial[(i + 1) * rows : (i + 2) * rows].astype(jnp.bfloat16)
        total = total + shifted(block, back).astype(jnp.float32)
    return total


def piece_table():
    depth, core = lax.axis_index("z"), lax.axis_index("core")
    along = [lax.rem(depth + 4 - step, 4) for step in (0,) + Z_STEPS]
    return jnp.stack([(core if own else 1 - core) * 4 + z for own in (True, False) for z in along])


def source_table():
    return jnp.stack([group_index(step, -1) for step in ((0, 0),) + SHIFTS])


def unit_kernel(piece_ref, gate_ref, up_ref, down_ref, out_ref):
    piece = piece_ref[0]
    real = (piece < UNIT_TILES) & (pl.program_id(0) * UNIT_TILES + piece < piece_ref[1])
    for i, ref in enumerate((gate_ref, up_ref, down_ref)):
        block = ref[...]
        out_ref[0, :, i * LANES : (i + 1) * LANES] = jnp.where(real, block, jnp.zeros_like(block))


def unit_pieces(w_gate, w_up, w_down):
    rows, units = w_gate.shape
    tiles = units // LANES
    piece = lax.axis_index("core") * 4 + lax.axis_index("z")
    numbers = jnp.stack([piece, jnp.int32(tiles)])
    spec = pl.BlockSpec(
        (rows, LANES), lambda j, num: (0, jnp.minimum(j * UNIT_TILES + num[0], tiles - 1))
    )
    return pl.pallas_call(
        unit_kernel,
        out_shape=jax.ShapeDtypeStruct((8, rows, 3 * LANES), jnp.bfloat16),
        grid_spec=pltpu.PrefetchScalarGridSpec(
            num_scalar_prefetch=1,
            grid=(8,),
            in_specs=[spec] * 3,
            out_specs=pl.BlockSpec((1, rows, 3 * LANES), lambda j, num: (j, 0, 0)),
        ),
    )(numbers, w_gate, w_up, w_down)


def unit_shards(pieces):
    me = group_index()
    stack = place(jnp.zeros_like(pieces), pick(pieces, me), me)
    for step in SHIFTS:
        block = shifted(pick(pieces, group_index(step)), step)
        stack = place(stack, block, group_index(step, -1))
    stack = stack.reshape(-1, 3 * LANES)
    mine = [stack] + [turned(stack, "z", step, 4) for step in Z_STEPS]
    other = swapped(jnp.stack(mine), "core")
    slots = mine + [other[i] for i in range(4)]
    return tuple(
        jnp.concatenate([slot[:, i * LANES : (i + 1) * LANES] for slot in slots], axis=1)
        for i in range(3)
    )


def plus(*blocks):
    return sum(block.astype(jnp.float32) for block in blocks).astype(jnp.bfloat16)


def assemble_units_kernel(table_ref, mine_ref, other_ref, *out_refs):
    for slot in range(8):
        held = mine_ref if slot < 4 else other_ref
        piece = table_ref[slot]

        @pl.when(piece < UNIT_TILES)
        def _():
            cols = pl.ds(pl.multiple_of(piece * LANES, LANES), LANES)
            for i, out_ref in enumerate(out_refs):
                block = held[slot % 4, 0, :, i * LANES : (i + 1) * LANES]
                out_ref[:, cols] = block.astype(jnp.float32)


def assemble_units(mine, other, units):
    rows = mine.shape[2]
    table = jnp.concatenate([piece_table(), source_table()])
    block = UNIT_TILES * LANES
    spec = pl.BlockSpec((4, 1, rows, 3 * LANES), lambda r, table: (0, r, 0, 0))
    return pl.pallas_call(
        assemble_units_kernel,
        out_shape=[jax.ShapeDtypeStruct((rows, units), jnp.float32)] * 3,
        grid_spec=pltpu.PrefetchScalarGridSpec(
            num_scalar_prefetch=1,
            grid=(8,),
            in_specs=[spec] * 2,
            out_specs=[pl.BlockSpec((rows, block), lambda r, table: (0, table[8 + r]))] * 3,
        ),
        compiler_params=pltpu.CompilerParams(vmem_limit_bytes=32 * 2**20),
    )(table, mine, other)


def assemble_attn_kernel(table_ref, mine_ref, other_ref, query_ref, out_ref, pair_ref):
    for slot in range(8):
        held = mine_ref if slot < 4 else other_ref
        piece = table_ref[slot]
        cols = pl.ds(pl.multiple_of(piece * LANES, LANES), LANES)
        block = held[slot % 4].astype(jnp.float32)
        query_ref[:, cols] = block[:, :LANES]
        out_ref[:, cols] = block[:, LANES : 2 * LANES]

        @pl.when(piece < 4)
        def _():
            pair_ref[:, cols] = block[:, 2 * LANES :]


def assemble_attn(mine, other):
    rows = mine.shape[1]
    return pl.pallas_call(
        assemble_attn_kernel,
        out_shape=[
            jax.ShapeDtypeStruct((rows, width * LANES), jnp.float32) for width in (8, 8, 4)
        ],
        in_specs=[pl.BlockSpec(memory_space=pltpu.SMEM)]
        + [pl.BlockSpec(memory_space=pltpu.VMEM)] * 2,
        out_specs=[pl.BlockSpec(memory_space=pltpu.VMEM)] * 3,
        compiler_params=pltpu.CompilerParams(vmem_limit_bytes=32 * 2**20),
    )(piece_table(), mine, other)


def to_slots(grad):
    return jnp.transpose(grad.reshape(grad.shape[0], -1, LANES), (1, 0, 2))


def unit_grads(grad_gate, grad_up, grad_down, units):
    slots = jnp.concatenate([to_slots(g) for g in (grad_gate, grad_up, grad_down)], axis=2)
    mine, other = slots[:4], slots[4:]
    total = plus(mine, swapped(other, "core"))
    total = plus(
        total[0],
        *[turned(total[1 + i], "z", (4 - step) % 4, 4) for i, step in enumerate(Z_STEPS)],
    )
    total = total.reshape(8, 144, 3 * LANES)
    blocks = [pick(total, group_index())]
    blocks += [shifted(pick(total, group_index(step)), step) for step in SHIFTS]
    stack = jnp.stack(blocks)
    stack = plus(stack, swapped(stack, "yl"))
    mine = jnp.stack([stack] + [turned(stack, "z", step, 4) for step in Z_STEPS])
    return assemble_units(mine, swapped(mine, "core"), units)


def attn_grads_of(grad_projected, grad_out):
    query, pair = grad_projected[:, :1024], grad_projected[:, 1024:]
    pair = jnp.pad(pair, ((0, 0), (0, 512)))
    slots = jnp.concatenate([to_slots(g) for g in (query, grad_out, pair)], axis=2)
    core, depth = lax.axis_index("core"), lax.axis_index("z")
    halves = slots.reshape((2, 4) + slots.shape[1:])
    total = plus(pick(halves, core), swapped(pick(halves, 1 - core), "core"))
    total = plus(
        pick(total, depth),
        *[turned(pick(total, lax.rem(depth + step, 4)), "z", step, 4) for step in Z_STEPS],
    )
    total = total.reshape(8, 144, 3 * LANES)
    total = plus(
        pick(total, group_index()),
        *[shifted(pick(total, group_index(step)), step) for step in SHIFTS],
    )
    total = plus(total, swapped(total, "yl"))
    mine = jnp.stack([total] + [turned(total, "z", step, 4) for step in Z_STEPS])
    return assemble_attn(mine, swapped(mine, "core"))


def total_vector(vector):
    for axis in ("core", "yl", "yh"):
        vector = vector + swapped(vector, axis)
    for axis in ("z", "x"):
        for flip in (1, 2):
            vector = vector + lax.ppermute(vector, axis, [(i, i ^ flip) for i in range(4)])
    return vector


def norm_rows(entries, gain_row):
    return (
        entries
        * lax.rsqrt(jnp.mean(entries * entries, axis=-1, keepdims=True) + EPSILON)
        * gain_row
    )


def turn_tables(position_rows, head_width):
    half_width = head_width // 2
    frequency = ROPE_BASE ** (-2.0 * jnp.arange(half_width, dtype=jnp.float32) / head_width)
    angles = position_rows.astype(jnp.float32)[..., None] * frequency
    return (jnp.cos(angles), jnp.sin(angles))


def rotate(entries, cosine_table, sine_table):
    half_width = entries.shape[-1] // 2
    leading = entries[..., :half_width]
    trailing = entries[..., half_width:]
    return jnp.concatenate(
        [
            leading * cosine_table - trailing * sine_table,
            trailing * cosine_table + leading * sine_table,
        ],
        axis=-1,
    )


def query_piece(raw_proj, gain_row, cosine_table, sine_table):
    head_width = gain_row.shape[0]
    shaped = raw_proj.reshape(cosine_table.shape[0], cosine_table.shape[1], -1, head_width)
    turned = rotate(
        norm_rows(shaped, gain_row), cosine_table[:, :, None, :], sine_table[:, :, None, :]
    )
    return jnp.transpose(turned, (0, 2, 1, 3)) * head_width ** (-0.5)


def key_piece(raw_proj, gain_row, cosine_table, sine_table):
    shaped = raw_proj.reshape(cosine_table.shape[0], cosine_table.shape[1], gain_row.shape[0])
    return rotate(norm_rows(shaped, gain_row), cosine_table, sine_table)


def gelu_product(gate_proj, up_proj):
    return jax.nn.gelu(gate_proj, approximate=True) * up_proj


def masked_scores(queries, key_rows, allowed):
    plain = jnp.einsum("shqd,skd->shqk", queries, key_rows, preferred_element_type=jnp.float32)
    return jnp.where(allowed, plain, MASKED)


def transposed_product(left_side, right_side):
    return lax.dot_general(left_side, right_side, CONTRACT_ROWS, preferred_element_type=jnp.float32)


def product_by_rows(left_side, right_side):
    return lax.dot_general(left_side, right_side, CONTRACT_COLS, preferred_element_type=jnp.float32)


def local(
    tokens,
    positions,
    cotangent,
    gain_attn,
    gain_query,
    gain_key,
    gain_post_attn,
    gain_ffn,
    gain_post_ffn,
    w_query,
    w_key,
    w_value,
    w_out,
    w_gate,
    w_up,
    w_down,
):
    seq_count, tok_rows, model_width = tokens.shape
    all_rows = seq_count * tok_rows
    head_width = gain_query.shape[0]
    query_cols = w_query.shape[1]
    reach_back = min(-(-(WINDOW - 1) // tok_rows), 7)
    cosine_table, sine_table = turn_tables(positions, head_width)
    inputs = tokens.astype(jnp.float32).reshape(all_rows, model_width)
    normed_full, norm_attn_back = jax.vjp(norm_rows, inputs, gain_attn)
    normed = normed_full.astype(jnp.bfloat16)
    qkv_held = by_core(
        w_query[:, :768], jnp.concatenate([w_query[:, 768:], w_key, w_value], axis=1)
    )
    qkv_rows = lax.all_to_all(jnp.broadcast_to(qkv_held, (8,) + qkv_held.shape), GROUP, 0, 0)
    unit_held = unit_pieces(w_gate, w_up, w_down)
    qkv_first, qkv_second = core_pair(qkv_rows.reshape(model_width, -1))
    out_held = by_core(w_out[:, :512], w_out[:, 512:])
    out_held, unit_held, _ = lax.optimization_barrier((out_held, unit_held, qkv_rows))
    out_rows = gather_rows(out_held)
    out_first, out_second = core_pair(out_rows)
    unit_held, _ = lax.optimization_barrier((unit_held, out_rows))
    gate_cols, up_cols, down_cols = unit_shards(unit_held)
    first_raw = jnp.dot(normed, qkv_first, preferred_element_type=jnp.float32)
    second_raw = jnp.dot(normed, qkv_second, preferred_element_type=jnp.float32)
    query_raw = jnp.concatenate([first_raw, second_raw[:, :256]], axis=1)
    key_raw = second_raw[:, 256:512]
    value_raw = second_raw[:, 512:]

    def query_local(raw_proj, gain_row):
        return query_piece(raw_proj, gain_row, cosine_table, sine_table)

    def key_local(raw_proj, gain_row):
        return key_piece(raw_proj, gain_row, cosine_table, sine_table)

    queries_full, query_back = jax.vjp(query_local, query_raw, gain_query)
    keys_full, key_back = jax.vjp(key_local, key_raw, gain_key)
    queries = queries_full.astype(jnp.bfloat16)
    local_pairs = jnp.concatenate(
        [keys_full, value_raw.reshape(seq_count, tok_rows, head_width)], axis=-1
    ).astype(jnp.bfloat16)
    collected = [local_pairs]
    for distance in range(1, reach_back + 1):
        collected.insert(0, from_behind(local_pairs, distance))
    pair_rows = jnp.concatenate(collected, axis=1)
    key_rows = pair_rows[..., :head_width]
    value_rows = pair_rows[..., head_width:]
    place_index = group_index()
    query_index = place_index * tok_rows + jnp.arange(tok_rows, dtype=jnp.int32)
    key_index = (place_index - reach_back) * tok_rows + jnp.arange(
        (reach_back + 1) * tok_rows, dtype=jnp.int32
    )
    offsets = query_index[:, None] - key_index[None, :]
    doc_start = query_index[None, :] - positions
    allowed = ((offsets >= 0) & (offsets < WINDOW))[None, :, :] & (
        key_index[None, None, :] >= doc_start[:, :, None]
    )
    allowed = allowed[:, None, :, :]
    scores = masked_scores(queries, key_rows, allowed)
    highest = jnp.max(scores, axis=-1, keepdims=True)
    exp_scores = jnp.exp(scores - highest)
    sum_scores = jnp.sum(exp_scores, axis=-1, keepdims=True)
    log_total = highest + jnp.log(sum_scores)
    weights = (exp_scores / sum_scores).astype(jnp.bfloat16)
    mixed_heads = jnp.einsum(
        "shqk,skd->sqhd", weights, value_rows, preferred_element_type=jnp.float32
    )
    attended = mixed_heads.reshape(all_rows, query_cols).astype(jnp.bfloat16)
    attn_branch = product_by_rows(attended[:, :512], out_first) + product_by_rows(
        attended[:, 512:], out_second
    )
    attn_normed, norm_post_attn_back = jax.vjp(norm_rows, attn_branch, gain_post_attn)
    middle = inputs + attn_normed
    ffn_in_full, norm_ffn_back = jax.vjp(norm_rows, middle, gain_ffn)
    normed_ffn = ffn_in_full.astype(jnp.bfloat16)
    ffn_rows = gather_tokens(normed_ffn)
    gate_proj = jnp.dot(ffn_rows, gate_cols, preferred_element_type=jnp.float32)
    up_proj = jnp.dot(ffn_rows, up_cols, preferred_element_type=jnp.float32)
    hidden_full, gelu_back = jax.vjp(gelu_product, gate_proj, up_proj)
    hidden = hidden_full.astype(jnp.bfloat16)
    ffn_branch = scatter_tokens(product_by_rows(hidden, down_cols))
    ffn_normed, norm_post_ffn_back = jax.vjp(norm_rows, ffn_branch, gain_post_ffn)
    outputs = (middle + ffn_normed).astype(jnp.bfloat16).reshape(seq_count, tok_rows, model_width)
    upstream = cotangent.astype(jnp.float32).reshape(all_rows, model_width)
    grad_ffn_branch, grad_post_ffn = norm_post_ffn_back(upstream)
    grad_ffn_branch = grad_ffn_branch.astype(jnp.bfloat16)
    grad_branch_rows = gather_tokens(grad_ffn_branch)
    grad_hidden = jnp.dot(grad_branch_rows, down_cols, preferred_element_type=jnp.float32)
    grad_gate_full, grad_up_full = gelu_back(grad_hidden)
    grad_gate_part = grad_gate_full.astype(jnp.bfloat16)
    grad_up_part = grad_up_full.astype(jnp.bfloat16)
    grad_normed_ffn = scatter_tokens(
        product_by_rows(grad_gate_part, gate_cols) + product_by_rows(grad_up_part, up_cols)
    )
    grad_gate_total, grad_up_total, grad_down_total = unit_grads(
        transposed_product(ffn_rows, grad_gate_part).astype(jnp.bfloat16),
        transposed_product(ffn_rows, grad_up_part).astype(jnp.bfloat16),
        transposed_product(grad_branch_rows, hidden).astype(jnp.bfloat16),
        w_gate.shape[1],
    )
    grad_middle_part, grad_gain_ffn = norm_ffn_back(grad_normed_ffn)
    grad_middle = upstream + grad_middle_part
    grad_attn_branch, grad_post_attn = norm_post_attn_back(grad_middle)
    grad_attn_branch = grad_attn_branch.astype(jnp.bfloat16)
    grad_attended = jnp.concatenate(
        [
            jnp.dot(grad_attn_branch, out_first, preferred_element_type=jnp.float32),
            jnp.dot(grad_attn_branch, out_second, preferred_element_type=jnp.float32),
        ],
        axis=1,
    )
    grad_heads = grad_attended.astype(jnp.bfloat16).reshape(seq_count, tok_rows, HEADS, head_width)
    scores = masked_scores(queries, key_rows, allowed)
    probabilities = jnp.exp(scores - log_total)
    grad_probs = jnp.einsum(
        "sqhd,skd->shqk", grad_heads, value_rows, preferred_element_type=jnp.float32
    )
    centre = jnp.sum(probabilities * grad_probs, axis=-1, keepdims=True)
    grad_scores = (probabilities * (grad_probs - centre)).astype(jnp.bfloat16)
    grad_queries = jnp.einsum(
        "shqk,skd->shqd", grad_scores, key_rows, preferred_element_type=jnp.float32
    )
    grad_key_rows = jnp.einsum(
        "shqk,shqd->skd", grad_scores, queries, preferred_element_type=jnp.float32
    )
    grad_value_rows = jnp.einsum(
        "shqk,sqhd->skd",
        probabilities.astype(jnp.bfloat16),
        grad_heads,
        preferred_element_type=jnp.float32,
    )
    grad_pairs = jnp.concatenate([grad_key_rows, grad_value_rows], axis=-1)
    own_pairs = grad_pairs[:, reach_back * tok_rows :]
    for distance in range(1, reach_back + 1):
        lower_block = reach_back - distance
        sent_block = grad_pairs[:, lower_block * tok_rows : (lower_block + 1) * tok_rows]
        own_pairs = own_pairs + from_behind(
            sent_block.astype(jnp.bfloat16), -distance
        ).astype(sent_block.dtype)
    grad_key_raw, grad_gain_key = key_back(own_pairs[..., :head_width])
    grad_query_raw, grad_gain_query = query_back(grad_queries)
    grad_value_raw = own_pairs[..., head_width:].reshape(all_rows, head_width)
    grad_projected = jnp.concatenate([grad_query_raw, grad_key_raw, grad_value_raw], axis=1).astype(
        jnp.bfloat16
    )
    contribution = product_by_rows(grad_projected[:, :768], qkv_first) + product_by_rows(
        grad_projected[:, 768:], qkv_second
    )
    query_total, grad_out_total, pair_total = attn_grads_of(
        transposed_product(normed, grad_projected).astype(jnp.bfloat16),
        transposed_product(grad_attn_branch, attended).astype(jnp.bfloat16),
    )
    grad_inputs_part, grad_gain_attn = norm_attn_back(contribution)
    grad_tokens = (grad_middle + grad_inputs_part).reshape(seq_count, tok_rows, model_width)
    gains = total_vector(
        jnp.concatenate(
            [
                grad_gain_attn,
                grad_gain_query,
                grad_gain_key,
                grad_post_attn,
                grad_gain_ffn,
                grad_post_ffn,
            ]
        )
    )
    query_at, key_at = model_width, model_width + head_width
    wide_at = key_at + head_width
    return (
        outputs,
        grad_tokens,
        gains[:query_at],
        gains[query_at:key_at],
        gains[key_at:wide_at],
        gains[wide_at : wide_at + model_width],
        gains[wide_at + model_width : wide_at + 2 * model_width],
        gains[wide_at + 2 * model_width :],
        query_total,
        pair_total[:, :head_width],
        pair_total[:, head_width:],
        grad_out_total,
        grad_gate_total,
        grad_up_total,
        grad_down_total,
    )


def solution(mesh):
    fine = Mesh(mesh.devices.reshape(4, 2, 4, 2, 2), GROUP + REPLICA)
    placed = (
        P(REPLICA, GROUP, None),
        P(REPLICA, GROUP),
        P(REPLICA, GROUP, None),
        P(),
        P(),
        P(),
        P(),
        P(),
        P(),
        P(GROUP, None),
        P(GROUP, None),
        P(GROUP, None),
        P(GROUP, None),
        P(GROUP, None),
        P(GROUP, None),
        P(GROUP, None),
    )
    return jax.shard_map(
        local,
        mesh=fine,
        in_specs=placed,
        out_specs=(
            P(REPLICA, GROUP, None),
            P(REPLICA, GROUP, None),
            P(),
            P(),
            P(),
            P(),
            P(),
            P(),
            P(GROUP, None),
            P(GROUP, None),
            P(GROUP, None),
            P(GROUP, None),
            P(GROUP, None),
            P(GROUP, None),
            P(GROUP, None),
        ),
        check_vma=False,
    )
```

time: 1540 us -> 632 us (0.41)
  waiting for transfers between devices: 1170 us -> 207 us
  starting transfers between devices: 18.3 us -> 230 us
  blocking collectives: 131 us -> 0 us
  matrix products: 112 us -> 62 us
  local copies, waits for them, and re-layouts: 21.6 us -> 68.6 us
  Pallas kernels: 0 us -> 16.1 us
    all_gather x5 -> x0, waiting for transfers between devices: 553 us -> none  [the longest x1 176 us: local(): lax.all_gather(w_gate, 'group', axis=0, tiled=True)]
    reduce_scatter x2 -> x0, waiting for transfers between devices: 517 us -> none  [the longest x1 472 us: local(): lax.psum_scatter(jnp.concatenate([transposed_product(normed_ffn, grad_uni...]
    ppermute x8 -> x95, starting transfers between devices: 18 us -> 222 us  [the longest x56 116 us: shifted(): return lax.ppermute(block, GROUP, route)]
    ppermute x8 -> x95, waiting for transfers between devices: 4.97 us -> 188 us  [the longest x27 113 us: turned(): lax.ppermute(block, axis, [(i, (i + step) % size) for i in range(size)])]
    psum x1 -> x0, waiting for transfers between devices: 95.1 us -> none  [replica_total(): lax.psum(shards[1].astype(jnp.bfloat16), 'replica').astype(jnp.float32)]
    psum x1 -> x0, blocking collectives: 68.6 us -> none  [local(): lax.psum((grad_gain_attn, grad_gain_query, grad_gain_key, grad_post_attn,...]
    all_gather x2 -> x0, blocking collectives: 61.9 us -> none  [the longest x1 31.3 us: local(): lax.all_gather(w_key, 'group', axis=0, tiled=True)]
    concatenate x2 -> x4, other arithmetic: 35.7 us -> 5.09 us  [the longest x1 4 us: unit_grads(): jnp.concatenate([to_slots(g) for g in (grad_gate, grad_up, grad_down)], a...]
  transfers between devices with their start and end apart: 16 -> 96, of which waited for: 10 -> 39; matrix products, arithmetic and copies ran while one was open for 6% -> 17% of each run, Pallas kernels for 0% -> 1%
where the time goes in v1:
time: 632 us; the launch traced here: 622 us
  starting transfers between devices  230 us (36%)
  waiting for transfers between devices  207 us (33%)
  local copies, waits for them, and re-layouts  68.6 us (11%)
  matrix products  62 us (10%)
  other arithmetic  37 us (6%)
  Pallas kernels  16.1 us (3%)
    ppermute x56, starting transfers between devices, shifted(): return lax.ppermute(block, GROUP, route)  116 us
    ppermute x27, waiting for transfers between devices, turned(): lax.ppermute(block, axis, [(i, (i + step) % size) for i in range(size)])  113 us
    ppermute x27, starting transfers between devices, turned(): lax.ppermute(block, axis, [(i, (i + step) % size) for i in range(size)])  84 us
    ppermute x56, waiting for transfers between devices, shifted(): return lax.ppermute(block, GROUP, route)  61.9 us
    unnamed x198, local copies, waits for them, and re-layouts  23.2 us
    dot_general x7, matrix products, product_by_rows(): lax.dot_general(left_side, right_side, CONTRACT_COLS, preferred_element_t...  19 us
    all_to_all x1, waiting for transfers between devices, local(): lax.all_to_all(jnp.broadcast_to(qkv_held, (8,) + qkv_held.shape), GROUP,...  18.7 us
    dot_general x5, matrix products, transposed_product(): lax.dot_general(left_side, right_side, CONTRACT_ROWS, preferred_element_t...  18 us
  transfers between devices with their start and end apart: 96, of which 39 were waited for; matrix products, arithmetic and copies ran while one was open for 17% of the time, Pallas kernels for 1%

profile of v1, /device:TPU:1, one launch (start us, length us, event | category | flops | bytes accessed | tf_op | source)
XLA Modules:
  0.0 622.4 jit_solution(9808191449268059169)
XLA Ops:
  3.9 7.5 %all-to-all-start = ((bf16[8,144,768]{2,1,0:T(8,128)(2,1)}), bf16[8,144,768]{2,1,0:T(8,128)(2,1)}, u32[]{:S(2)}, u32[]{:S(2)}) async-start(bf16[8,144,768]{2,1,0:T(8,128)(2,1)} %broadcast_in_dim.119), calls=%async_computation | async-start | bytes 3538944 | tf_op jit(solution)/shard_map/all_to_all | solution.py:349
  12.0 5.6 shard_map.271
  18.5 18.7 %all-to-all-done = bf16[8,144,768]{2,1,0:T(8,128)(2,1)} async-done(((bf16[8,144,768]{2,1,0:T(8,128)(2,1)}), bf16[8,144,768]{2,1,0:T(8,128)(2,1)}, u32[]{:S(2)}, u32[]{:S(2)}) %all-to-all-start) | async-done | bytes 1769504 | tf_op jit(solution)/shard_map/all_to_all | solution.py:349
  41.4 4.7 collective-permute-start.9
  48.7 4.5 collective-permute-start.11
  63.4 3.9 collective-permute-start.24
  73.2 3.8 collective-permute-done.26
  82.5 6.8 %collective-permute-start = (bf16[1152,768]{1,0:T(8,128)(2,1)}, bf16[1152,768]{1,0:T(8,128)(2,1)S(1)}, u32[]{:S(2)}, u32[]{:S(2)}) collective-permute-start(bf16[1152,768]{1,0:T(8,128)(2,1)} %bitcast.2), channel_id=1, source_target_pairs={{0,1},{1,0},{2,3},{3,2},{4,5},{5,4},{6,7},{7,6},{8,9},{9,8},{10,11... | collective-permute-start | bytes 5308424 | tf_op jit(solution)/shard_map/ppermute | solution.py:40
  89.6 5.3 collective-permute-done.27
  94.9 19.9 %collective-permute-done.29 = bf16[1152,384]{1,0:T(8,128)(2,1)S(1)} collective-permute-done((bf16[1152,384]{1,0:T(8,128)(2,1)S(1)}, bf16[1152,384]{1,0:T(8,128)(2,1)S(1)}, u32[]{:S(2)}, u32[]{:S(2)}) %collective-permute-start.29) | collective-permute-done | bytes 884768 | tf_op jit(solution)/shard_map/ppermute | solution.py:40
  116.9 6.9 %collective-permute-start.30 = (bf16[4,1152,384]{2,1,0:T(8,128)(2,1)}, bf16[4,1152,384]{2,1,0:T(8,128)(2,1)}, u32[]{:S(2)}, u32[]{:S(2)}) collective-permute-start(bf16[4,1152,384]{2,1,0:T(8,128)(2,1)} %pad_maximum_fusion.2), channel_id=1, source_target_pairs={{0,1},{1,0},{2,3},{3,2},{4,5},{5,4},{6,7},{7,6},{8,9},{9,8},{10,11... | collective-permute-start | bytes 10616840 | tf_op jit(solution)/shard_map/ppermute | solution.py:40
  128.7 4.0 collective-permute-start.1
  167.5 11.2 %collective-permute-done.15 = bf16[128,1152]{1,0:T(8,128)(2,1)S(1)} collective-permute-done((bf16[128,1152]{1,0:T(8,128)(2,1)S(1)}, bf16[128,1152]{1,0:T(8,128)(2,1)S(1)}, u32[]{:S(2)}, u32[]{:S(2)}) %collective-permute-start.15) | collective-permute-done | bytes 294944 | tf_op jit(solution)/shard_map/ppermute | solution.py:36
  181.6 8.1 %collective-permute-done.19 = bf16[128,1152]{1,0:T(8,128)(2,1)S(1)} collective-permute-done((bf16[128,1152]{1,0:T(8,128)(2,1)S(1)}, bf16[128,1152]{1,0:T(8,128)(2,1)S(1)}, u32[]{:S(2)}, u32[]{:S(2)}) %collective-permute-start.19) | collective-permute-done | bytes 294944 | tf_op jit(solution)/shard_map/ppermute | solution.py:36
  197.5 5.1 multiply_convert_fusion.1
  219.4 9.9 %collective-permute-done.33 = bf16[128,1152]{1,0:T(8,128)(2,1)S(1)} collective-permute-done((bf16[128,1152]{1,0:T(8,128)(2,1)S(1)}, bf16[128,1152]{1,0:T(8,128)(2,1)S(1)}, u32[]{:S(2)}, u32[]{:S(2)}) %collective-permute-start.33) | collective-permute-done | bytes 294944 | tf_op jit(solution)/shard_map/ppermute | solution.py:36
  232.5 7.4 %collective-permute-done.37 = bf16[128,1152]{1,0:T(8,128)(2,1)S(1)} collective-permute-done((bf16[128,1152]{1,0:T(8,128)(2,1)S(1)}, bf16[128,1152]{1,0:T(8,128)(2,1)S(1)}, u32[]{:S(2)}, u32[]{:S(2)}) %collective-permute-start.37) | collective-permute-done | bytes 294944 | tf_op jit(solution)/shard_map/ppermute | solution.py:36
  246.8 5.0 collective-permute-start.42
  253.5 4.0 collective-permute-start.44
  264.4 3.8 collective-permute-done.44
  269.0 6.0 convolution_convert_fusion.2
  275.0 5.9 fusion.7
  281.0 4.3 convolution_convert_fusion.4
  288.2 4.6 fusion.137
  294.2 6.4 %collective-permute-start.45 = (bf16[128,1152]{1,0:T(8,128)(2,1)}, bf16[128,1152]{1,0:T(8,128)(2,1)}, u32[]{:S(2)}, u32[]{:S(2)}) collective-permute-start(bf16[128,1152]{1,0:T(8,128)(2,1)} %get-tuple-element.67), channel_id=1, source_target_pairs={{0,96},{16,112},{32,0},{48,16},{64,32},{80,48},{96,64},{112,80},{1... | collective-permute-start | bytes 884744 | tf_op jit(solution)/shard_map/ppermute | solution.py:36
  300.8 4.3 convolution_convert_fusion.3
  305.1 4.3 copy.129
  309.4 4.3 copy.127
  313.7 4.3 copy.128
  327.9 4.0 pad_maximum_fusion.1
  335.8 7.8 %collective-permute-start.79 = (bf16[4,1152,384]{2,1,0:T(8,128)(2,1)}, bf16[4,1152,384]{2,1,0:T(8,128)(2,1)}, u32[]{:S(2)}, u32[]{:S(2)}) collective-permute-start(bf16[4,1152,384]{2,1,0:T(8,128)(2,1)} %slice.428), channel_id=1, source_target_pairs={{0,1},{1,0},{2,3},{3,2},{4,5},{5,4},{6,7},{7,6},{8,9},{9,8},{10,11... | collective-permute-start | bytes 10616840 | tf_op jit(solution)/shard_map/ppermute | solution.py:40
  355.9 4.5 copy.125
  372.5 4.8 collective-permute-done.54
  400.3 5.8 collective-permute-start.63
  411.5 16.6 %collective-permute-done.82 = bf16[1152,384]{1,0:T(8,128)(2,1)} collective-permute-done((bf16[1152,384]{1,0:T(8,128)(2,1)}, bf16[1152,384]{1,0:T(8,128)(2,1)}, u32[]{:S(2)}, u32[]{:S(2)}) %collective-permute-start.82) | collective-permute-done | bytes 884768 | tf_op jit(solution)/shard_map/ppermute | solution.py:40
  430.7 4.7 collective-permute-start.83
  442.9 5.6 collective-permute-start.89
  448.5 3.6 collective-permute-done.89
  455.4 12.8 %collective-permute-done.90 = bf16[8,144,384]{2,1,0:T(8,128)(2,1)S(1)} collective-permute-done((bf16[8,144,384]{2,1,0:T(8,128)(2,1)S(1)}, bf16[8,144,384]{2,1,0:T(8,128)(2,1)S(1)}, u32[]{:S(2)}, u32[]{:S(2)}) %collective-permute-start.90) | collective-permute-done | bytes 884768 | tf_op jit(solution)/shard_map/ppermute | solution.py:40
  481.0 6.7 %collective-permute-done.91 = bf16[8,144,384]{2,1,0:T(8,128)(2,1)S(1)} collective-permute-done((bf16[8,144,384]{2,1,0:T(8,128)(2,1)S(1)}, bf16[8,144,384]{2,1,0:T(8,128)(2,1)S(1)}, u32[]{:S(2)}, u32[]{:S(2)}) %collective-permute-start.91) | collective-permute-done | bytes 884768 | tf_op jit(solution)/shard_map/ppermute | solution.py:40
  492.5 15.8 %collective-permute-done.93 = bf16[8,144,384]{2,1,0:T(8,128)(2,1)S(1)} collective-permute-done((bf16[8,144,384]{2,1,0:T(8,128)(2,1)S(1)}, bf16[8,144,384]{2,1,0:T(8,128)(2,1)S(1)}, u32[]{:S(2)}, u32[]{:S(2)}) %collective-permute-start.93) | collective-permute-done | bytes 884768 | tf_op jit(solution)/shard_map/ppermute | solution.py:40
  508.9 16.7 %collective-permute-start.94 = (bf16[4,8,144,384]{3,2,1,0:T(8,128)(2,1)S(1)}, bf16[4,8,144,384]{3,2,1,0:T(8,128)(2,1)}, u32[]{:S(2)}, u32[]{:S(2)}) collective-permute-start(bf16[4,8,144,384]{3,2,1,0:T(8,128)(2,1)S(1)} %pad_maximum_fusion.3.mine_ref), channel_id=1, source_target_pairs={{0,1},{1,0},{2,3},{3,2},{4,5},{5,4},{6,7},{7,6},{8,9},{9,8},{10,11... | collective-permute-start | bytes 10616840 | tf_op jit(solution)/shard_map/ppermute | solution.py:40
  525.8 20.4 %collective-permute-done.66 = bf16[1152,384]{1,0:T(8,128)(2,1)S(1)} collective-permute-done((bf16[1152,384]{1,0:T(8,128)(2,1)S(1)}, bf16[1152,384]{1,0:T(8,128)(2,1)S(1)}, u32[]{:S(2)}, u32[]{:S(2)}) %collective-permute-start.66) | collective-permute-done | bytes 884768 | tf_op jit(solution)/shard_map/ppermute | solution.py:40
  552.7 6.8 %collective-permute-start.56 = (f32[5120]{0:T(1024)S(1)}, f32[5120]{0:T(1024)S(1)}, u32[]{:S(2)}, u32[]{:S(2)}) collective-permute-start(f32[5120]{0:T(1024)S(1)} %constant_dynamic-update-slice_fusion.30), channel_id=1, source_target_pairs={{0,1},{1,0},{2,3},{3,2},{4,5},{5,4},{6,7},{7,6},{8,9},{9,8},{10,11... | collective-permute-start | bytes 61448 | tf_op jit(solution)/shard_map/ppermute | solution.py:40
  574.5 5.0 collective-permute-start.71
  579.5 4.6 collective-permute-start.73
  602.2 7.4 %collective-permute-start.78 = (bf16[4,144,384]{2,1,0:T(8,128)(2,1)S(1)}, bf16[4,144,384]{2,1,0:T(8,128)(2,1)S(1)}, u32[]{:S(2)}, u32[]{:S(2)}) collective-permute-start(bf16[4,144,384]{2,1,0:T(8,128)(2,1)S(1)} %pad_maximum_fusion.6.mine_ref), channel_id=1, source_target_pairs={{0,1},{1,0},{2,3},{3,2},{4,5},{5,4},{6,7},{7,6},{8,9},{9,8},{10,11... | collective-permute-start | bytes 1327112 | tf_op jit(solution)/shard_map/ppermute | solution.py:40
  613.5 8.7 %shard_map.273 = (f32[144,6912]{1,0:T(8,128)}, f32[144,6912]{1,0:T(8,128)}, f32[144,6912]{1,0:T(8,128)}) custom-call(s32[16]{0:T(128)S(1)} %concatenate.91.table_ref, bf16[4,8,144,384]{3,2,1,0:T(8,128)(2,1)S(1)} %pad_maximum_fusion.3.mine_ref, bf16[4,8,144,384]{3,2,1,0:T(8,128)(2,1)} %collective-permute-done.94.other_ref), custom_call_target="tpu_custom_call" | custom-call | tf_op jit(solution)/shard_map/pallas_call | solution.py:168
  (498 shorter events, 266.8 us)
Async XLA Ops:
  3.9 33.3 %all-to-all-start = ((bf16[8,144,768]{2,1,0:T(8,128)(2,1)}), bf16[8,144,768]{2,1,0:T(8,128)(2,1)}, u32[]{:S(2)}, u32[]{:S(2)}) async-start(bf16[8,144,768]{2,1,0:T(8,128)(2,1)} %broadcast_in_dim.119), calls=%async_computation | async-start | bytes 3538944 | tf_op jit(solution)/shard_map/all_to_all | solution.py:349
  39.9 13.9 %collective-permute-start.7 = (bf16[144,512]{1,0:T(8,128)(2,1)S(1)}, bf16[144,512]{1,0:T(8,128)(2,1)S(1)}, u32[]{:S(2)}, u32[]{:S(2)}) collective-permute-start(bf16[144,512]{1,0:T(8,128)(2,1)S(1)} %slice_select_fusion), channel_id=1, source_target_pairs={{0,16},{16,0},{32,48},{48,32},{64,80},{80,64},{96,112},{112,96},{1... | collective-permute-start | bytes 442376 | tf_op jit(solution)/shard_map/ppermute | solution.py:36
  41.1 13.4 %collective-permute-start.8 = (bf16[144,512]{1,0:T(8,128)(2,1)S(1)}, bf16[144,512]{1,0:T(8,128)(2,1)S(1)}, u32[]{:S(2)}, u32[]{:S(2)}) collective-permute-start(bf16[144,512]{1,0:T(8,128)(2,1)S(1)} %slice_select_fusion), channel_id=1, source_target_pairs={{0,48},{16,32},{32,80},{48,64},{64,112},{80,96},{96,16},{112,0},{1... | collective-permute-start | bytes 442376 | tf_op jit(solution)/shard_map/ppermute | solution.py:36
  41.4 13.7 %collective-permute-start.9 = (bf16[144,512]{1,0:T(8,128)(2,1)S(1)}, bf16[144,512]{1,0:T(8,128)(2,1)S(1)}, u32[]{:S(2)}, u32[]{:S(2)}) collective-permute-start(bf16[144,512]{1,0:T(8,128)(2,1)S(1)} %slice_select_fusion), channel_id=1, source_target_pairs={{0,112},{16,96},{32,16},{48,0},{64,48},{80,32},{96,80},{112,64},{1... | collective-permute-start | bytes 442376 | tf_op jit(solution)/shard_map/ppermute | solution.py:36
  77.0 17.9 %collective-permute-start.27 = (bf16[1152,384]{1,0:T(8,128)(2,1)S(1)}, bf16[1152,384]{1,0:T(8,128)(2,1)S(1)}, u32[]{:S(2)}, u32[]{:S(2)}) collective-permute-start(bf16[1152,384]{1,0:T(8,128)(2,1)S(1)} %bitcast.321), channel_id=1, source_target_pairs={{0,4},{4,8},{8,12},{12,0},{1,5},{5,9},{9,13},{13,1},{2,6},{6,10},{... | collective-permute-start | bytes 2654216 | tf_op jit(solution)/shard_map/ppermute | solution.py:40
  78.7 16.2 %collective-permute-start.28 = (bf16[1152,384]{1,0:T(8,128)(2,1)S(1)}, bf16[1152,384]{1,0:T(8,128)(2,1)S(1)}, u32[]{:S(2)}, u32[]{:S(2)}) collective-permute-start(bf16[1152,384]{1,0:T(8,128)(2,1)S(1)} %bitcast.322), channel_id=1, source_target_pairs={{0,12},{4,0},{8,4},{12,8},{1,13},{5,1},{9,5},{13,9},{2,14},{6,2},{... | collective-permute-start | bytes 2654216 | tf_op jit(solution)/shard_map/ppermute | solution.py:40
  80.9 33.8 %collective-permute-start.29 = (bf16[1152,384]{1,0:T(8,128)(2,1)S(1)}, bf16[1152,384]{1,0:T(8,128)(2,1)S(1)}, u32[]{:S(2)}, u32[]{:S(2)}) collective-permute-start(bf16[1152,384]{1,0:T(8,128)(2,1)S(1)} %bitcast.323), channel_id=1, source_target_pairs={{0,8},{4,12},{8,0},{12,4},{1,9},{5,13},{9,1},{13,5},{2,10},{6,14},... | collective-permute-start | bytes 2654216 | tf_op jit(solution)/shard_map/ppermute | solution.py:40
  82.5 42.1 %collective-permute-start = (bf16[1152,768]{1,0:T(8,128)(2,1)}, bf16[1152,768]{1,0:T(8,128)(2,1)S(1)}, u32[]{:S(2)}, u32[]{:S(2)}) collective-permute-start(bf16[1152,768]{1,0:T(8,128)(2,1)} %bitcast.2), channel_id=1, source_target_pairs={{0,1},{1,0},{2,3},{3,2},{4,5},{5,4},{6,7},{7,6},{8,9},{9,8},{10,11... | collective-permute-start | bytes 5308424 | tf_op jit(solution)/shard_map/ppermute | solution.py:40
  89.3 58.4 %collective-permute-start.12 = (bf16[1152,512]{1,0:T(8,128)(2,1)}, bf16[1152,512]{1,0:T(8,128)(2,1)S(1)}, u32[]{:S(2)}, u32[]{:S(2)}) collective-permute-start(bf16[1152,512]{1,0:T(8,128)(2,1)} %bitcast.25), channel_id=1, source_target_pairs={{0,1},{1,0},{2,3},{3,2},{4,5},{5,4},{6,7},{7,6},{8,9},{9,8},{10,11... | collective-permute-start | bytes 3538952 | tf_op jit(solution)/shard_map/ppermute | solution.py:40
  116.9 72.9 %collective-permute-start.30 = (bf16[4,1152,384]{2,1,0:T(8,128)(2,1)}, bf16[4,1152,384]{2,1,0:T(8,128)(2,1)}, u32[]{:S(2)}, u32[]{:S(2)}) collective-permute-start(bf16[4,1152,384]{2,1,0:T(8,128)(2,1)} %pad_maximum_fusion.2), channel_id=1, source_target_pairs={{0,1},{1,0},{2,3},{3,2},{4,5},{5,4},{6,7},{7,6},{8,9},{9,8},{10,11... | collective-permute-start | bytes 10616840 | tf_op jit(solution)/shard_map/ppermute | solution.py:40
  156.4 22.3 %collective-permute-start.15 = (bf16[128,1152]{1,0:T(8,128)(2,1)S(1)}, bf16[128,1152]{1,0:T(8,128)(2,1)S(1)}, u32[]{:S(2)}, u32[]{:S(2)}) collective-permute-start(bf16[128,1152]{1,0:T(8,128)(2,1)S(1)} %get-tuple-element.52), channel_id=1, source_target_pairs={{0,16},{16,0},{32,48},{48,32},{64,80},{80,64},{96,112},{112,96},{1... | collective-permute-start | bytes 884744 | tf_op jit(solution)/shard_map/ppermute | solution.py:36
  160.0 21.5 %collective-permute-start.16 = (bf16[128,1152]{1,0:T(8,128)(2,1)S(1)}, bf16[128,1152]{1,0:T(8,128)(2,1)S(1)}, u32[]{:S(2)}, u32[]{:S(2)}) collective-permute-start(bf16[128,1152]{1,0:T(8,128)(2,1)S(1)} %get-tuple-element.52), channel_id=1, source_target_pairs={{0,48},{16,32},{32,80},{48,64},{64,112},{80,96},{96,16},{112,0},{1... | collective-permute-start | bytes 884744 | tf_op jit(solution)/shard_map/ppermute | solution.py:36
  163.6 18.0 %collective-permute-start.17 = (bf16[128,1152]{1,0:T(8,128)(2,1)S(1)}, bf16[128,1152]{1,0:T(8,128)(2,1)S(1)}, u32[]{:S(2)}, u32[]{:S(2)}) collective-permute-start(bf16[128,1152]{1,0:T(8,128)(2,1)S(1)} %get-tuple-element.52), channel_id=1, source_target_pairs={{0,112},{16,96},{32,16},{48,0},{64,48},{80,32},{96,80},{112,64},{1... | collective-permute-start | bytes 884744 | tf_op jit(solution)/shard_map/ppermute | solution.py:36
  165.9 15.7 %collective-permute-start.18 = (bf16[128,1152]{1,0:T(8,128)(2,1)S(1)}, bf16[128,1152]{1,0:T(8,128)(2,1)S(1)}, u32[]{:S(2)}, u32[]{:S(2)}) collective-permute-start(bf16[128,1152]{1,0:T(8,128)(2,1)S(1)} %get-tuple-element.52), channel_id=1, source_target_pairs={{0,64},{16,80},{32,96},{48,112},{64,0},{80,16},{96,32},{112,48},{1... | collective-permute-start | bytes 884744 | tf_op jit(solution)/shard_map/ppermute | solution.py:36
  208.4 20.9 %collective-permute-start.33 = (bf16[128,1152]{1,0:T(8,128)(2,1)S(1)}, bf16[128,1152]{1,0:T(8,128)(2,1)S(1)}, u32[]{:S(2)}, u32[]{:S(2)}) collective-permute-start(bf16[128,1152]{1,0:T(8,128)(2,1)S(1)} %get-tuple-element.79), channel_id=1, source_target_pairs={{0,16},{16,0},{32,48},{48,32},{64,80},{80,64},{96,112},{112,96},{1... | collective-permute-start | bytes 884744 | tf_op jit(solution)/shard_map/ppermute | solution.py:36
  211.7 17.6 %collective-permute-start.34 = (bf16[128,1152]{1,0:T(8,128)(2,1)S(1)}, bf16[128,1152]{1,0:T(8,128)(2,1)S(1)}, u32[]{:S(2)}, u32[]{:S(2)}) collective-permute-start(bf16[128,1152]{1,0:T(8,128)(2,1)S(1)} %get-tuple-element.78), channel_id=1, source_target_pairs={{0,112},{16,96},{32,16},{48,0},{64,48},{80,32},{96,80},{112,64},{1... | collective-permute-start | bytes 884744 | tf_op jit(solution)/shard_map/ppermute | solution.py:36
  213.8 15.6 %collective-permute-start.35 = (bf16[128,1152]{1,0:T(8,128)(2,1)S(1)}, bf16[128,1152]{1,0:T(8,128)(2,1)S(1)}, u32[]{:S(2)}, u32[]{:S(2)}) collective-permute-start(bf16[128,1152]{1,0:T(8,128)(2,1)S(1)} %get-tuple-element.77), channel_id=1, source_target_pairs={{0,48},{16,32},{32,80},{48,64},{64,112},{80,96},{96,16},{112,0},{1... | collective-permute-start | bytes 884744 | tf_op jit(solution)/shard_map/ppermute | solution.py:36
  215.6 16.9 %collective-permute-start.36 = (bf16[128,1152]{1,0:T(8,128)(2,1)S(1)}, bf16[128,1152]{1,0:T(8,128)(2,1)S(1)}, u32[]{:S(2)}, u32[]{:S(2)}) collective-permute-start(bf16[128,1152]{1,0:T(8,128)(2,1)S(1)} %get-tuple-element.76), channel_id=1, source_target_pairs={{0,64},{16,80},{32,96},{48,112},{64,0},{80,16},{96,32},{112,48},{1... | collective-permute-start | bytes 884744 | tf_op jit(solution)/shard_map/ppermute | solution.py:36
  216.4 23.4 %collective-permute-start.37 = (bf16[128,1152]{1,0:T(8,128)(2,1)S(1)}, bf16[128,1152]{1,0:T(8,128)(2,1)S(1)}, u32[]{:S(2)}, u32[]{:S(2)}) collective-permute-start(bf16[128,1152]{1,0:T(8,128)(2,1)S(1)} %get-tuple-element.75), channel_id=1, source_target_pairs={{0,80},{16,64},{32,112},{48,96},{64,16},{80,0},{96,48},{112,32},{1... | collective-permute-start | bytes 884744 | tf_op jit(solution)/shard_map/ppermute | solution.py:36
  244.9 13.3 %collective-permute-start.40 = (bf16[128,1152]{1,0:T(8,128)(2,1)}, bf16[128,1152]{1,0:T(8,128)(2,1)S(1)}, u32[]{:S(2)}, u32[]{:S(2)}) collective-permute-start(bf16[128,1152]{1,0:T(8,128)(2,1)} %get-tuple-element.48), channel_id=1, source_target_pairs={{0,16},{16,0},{32,48},{48,32},{64,80},{80,64},{96,112},{112,96},{1... | collective-permute-start | bytes 884744 | tf_op jit(solution)/shard_map/ppermute | solution.py:36
  246.6 13.3 %collective-permute-start.41 = (bf16[128,1152]{1,0:T(8,128)(2,1)}, bf16[128,1152]{1,0:T(8,128)(2,1)S(1)}, u32[]{:S(2)}, u32[]{:S(2)}) collective-permute-start(bf16[128,1152]{1,0:T(8,128)(2,1)} %get-tuple-element.48), channel_id=1, source_target_pairs={{0,48},{16,32},{32,80},{48,64},{64,112},{80,96},{96,16},{112,0},{1... | collective-permute-start | bytes 884744 | tf_op jit(solution)/shard_map/ppermute | solution.py:36
  246.8 13.8 %collective-permute-start.42 = (bf16[128,1152]{1,0:T(8,128)(2,1)}, bf16[128,1152]{1,0:T(8,128)(2,1)S(1)}, u32[]{:S(2)}, u32[]{:S(2)}) collective-permute-start(bf16[128,1152]{1,0:T(8,128)(2,1)} %get-tuple-element.48), channel_id=1, source_target_pairs={{0,112},{16,96},{32,16},{48,0},{64,48},{80,32},{96,80},{112,64},{1... | collective-permute-start | bytes 884744 | tf_op jit(solution)/shard_map/ppermute | solution.py:36
  253.5 14.7 %collective-permute-start.44 = (bf16[128,1152]{1,0:T(8,128)(2,1)}, bf16[128,1152]{1,0:T(8,128)(2,1)S(1)}, u32[]{:S(2)}, u32[]{:S(2)}) collective-permute-start(bf16[128,1152]{1,0:T(8,128)(2,1)} %get-tuple-element.48), channel_id=1, source_target_pairs={{0,80},{16,64},{32,112},{48,96},{64,16},{80,0},{96,48},{112,32},{1... | collective-permute-start | bytes 884744 | tf_op jit(solution)/shard_map/ppermute | solution.py:36
  294.2 29.5 %collective-permute-start.45 = (bf16[128,1152]{1,0:T(8,128)(2,1)}, bf16[128,1152]{1,0:T(8,128)(2,1)}, u32[]{:S(2)}, u32[]{:S(2)}) collective-permute-start(bf16[128,1152]{1,0:T(8,128)(2,1)} %get-tuple-element.67), channel_id=1, source_target_pairs={{0,96},{16,112},{32,0},{48,16},{64,32},{80,48},{96,64},{112,80},{1... | collective-permute-start | bytes 884744 | tf_op jit(solution)/shard_map/ppermute | solution.py:36
  300.6 24.2 %collective-permute-start.46 = (bf16[128,1152]{1,0:T(8,128)(2,1)}, bf16[128,1152]{1,0:T(8,128)(2,1)}, u32[]{:S(2)}, u32[]{:S(2)}) collective-permute-start(bf16[128,1152]{1,0:T(8,128)(2,1)} %get-tuple-element.73), channel_id=1, source_target_pairs={{0,32},{16,48},{32,64},{48,80},{64,96},{80,112},{96,0},{112,16},{1... | collective-permute-start | bytes 884744 | tf_op jit(solution)/shard_map/ppermute | solution.py:36
  317.9 17.9 %collective-permute-start.47 = (bf16[128,1152]{1,0:T(8,128)(2,1)}, bf16[128,1152]{1,0:T(8,128)(2,1)S(1)}, u32[]{:S(2)}, u32[]{:S(2)}) collective-permute-start(bf16[128,1152]{1,0:T(8,128)(2,1)} %get-tuple-element.72), channel_id=1, source_target_pairs={{0,16},{16,0},{32,48},{48,32},{64,80},{80,64},{96,112},{112,96},{1... | collective-permute-start | bytes 884744 | tf_op jit(solution)/shard_map/ppermute | solution.py:36
  319.8 23.8 %collective-permute-start.48 = (bf16[128,1152]{1,0:T(8,128)(2,1)}, bf16[128,1152]{1,0:T(8,128)(2,1)S(1)}, u32[]{:S(2)}, u32[]{:S(2)}) collective-permute-start(bf16[128,1152]{1,0:T(8,128)(2,1)} %get-tuple-element.71), channel_id=1, source_target_pairs={{0,112},{16,96},{32,16},{48,0},{64,48},{80,32},{96,80},{112,64},{1... | collective-permute-start | bytes 884744 | tf_op jit(solution)/shard_map/ppermute | solution.py:36
  323.3 20.3 %collective-permute-start.49 = (bf16[128,1152]{1,0:T(8,128)(2,1)}, bf16[128,1152]{1,0:T(8,128)(2,1)S(1)}, u32[]{:S(2)}, u32[]{:S(2)}) collective-permute-start(bf16[128,1152]{1,0:T(8,128)(2,1)} %get-tuple-element.70), channel_id=1, source_target_pairs={{0,48},{16,32},{32,80},{48,64},{64,112},{80,96},{96,16},{112,0},{1... | collective-permute-start | bytes 884744 | tf_op jit(solution)/shard_map/ppermute | solution.py:36
  323.7 19.9 %collective-permute-start.50 = (bf16[128,1152]{1,0:T(8,128)(2,1)}, bf16[128,1152]{1,0:T(8,128)(2,1)S(1)}, u32[]{:S(2)}, u32[]{:S(2)}) collective-permute-start(bf16[128,1152]{1,0:T(8,128)(2,1)} %get-tuple-element.69), channel_id=1, source_target_pairs={{0,64},{16,80},{32,96},{48,112},{64,0},{80,16},{96,32},{112,48},{1... | collective-permute-start | bytes 884744 | tf_op jit(solution)/shard_map/ppermute | solution.py:36
  324.9 18.8 %collective-permute-start.51 = (bf16[128,1152]{1,0:T(8,128)(2,1)}, bf16[128,1152]{1,0:T(8,128)(2,1)S(1)}, u32[]{:S(2)}, u32[]{:S(2)}) collective-permute-start(bf16[128,1152]{1,0:T(8,128)(2,1)} %get-tuple-element.68), channel_id=1, source_target_pairs={{0,80},{16,64},{32,112},{48,96},{64,16},{80,0},{96,48},{112,32},{1... | collective-permute-start | bytes 884744 | tf_op jit(solution)/shard_map/ppermute | solution.py:36
  335.8 49.1 %collective-permute-start.79 = (bf16[4,1152,384]{2,1,0:T(8,128)(2,1)}, bf16[4,1152,384]{2,1,0:T(8,128)(2,1)}, u32[]{:S(2)}, u32[]{:S(2)}) collective-permute-start(bf16[4,1152,384]{2,1,0:T(8,128)(2,1)} %slice.428), channel_id=1, source_target_pairs={{0,1},{1,0},{2,3},{3,2},{4,5},{5,4},{6,7},{7,6},{8,9},{9,8},{10,11... | collective-permute-start | bytes 10616840 | tf_op jit(solution)/shard_map/ppermute | solution.py:40
  363.8 13.5 %collective-permute-start.54 = (bf16[1,128,512]{2,1,0:T(8,128)(2,1)}, bf16[1,128,512]{2,1,0:T(8,128)(2,1)}, u32[]{:S(2)}, u32[]{:S(2)}) collective-permute-start(bf16[1,128,512]{2,1,0:T(8,128)(2,1)} %get-tuple-element.132), channel_id=1, source_target_pairs={{48,0},{64,16},{80,32},{96,48},{112,64},{49,1},{65,17},{81,33},{97... | collective-permute-start | bytes 393224 | tf_op jit(solution)/shard_map/ppermute | solution.py:31
  365.1 13.1 %collective-permute-start.55 = (bf16[1,128,512]{2,1,0:T(8,128)(2,1)}, bf16[1,128,512]{2,1,0:T(8,128)(2,1)}, u32[]{:S(2)}, u32[]{:S(2)}) collective-permute-start(bf16[1,128,512]{2,1,0:T(8,128)(2,1)} %get-tuple-element.131), channel_id=1, source_target_pairs={{64,0},{80,16},{96,32},{112,48},{65,1},{81,17},{97,33},{113,49},{6... | collective-permute-start | bytes 393224 | tf_op jit(solution)/shard_map/ppermute | solution.py:31
  391.8 16.3 %collective-permute-start.80 = (bf16[1152,384]{1,0:T(8,128)(2,1)}, bf16[1152,384]{1,0:T(8,128)(2,1)}, u32[]{:S(2)}, u32[]{:S(2)}) collective-permute-start(bf16[1152,384]{1,0:T(8,128)(2,1)} %get-tuple-element.57), channel_id=1, source_target_pairs={{0,12},{4,0},{8,4},{12,8},{1,13},{5,1},{9,5},{13,9},{2,14},{6,2},{... | collective-permute-start | bytes 2654216 | tf_op jit(solution)/shard_map/ppermute | solution.py:40
  393.2 18.3 %collective-permute-start.81 = (bf16[1152,384]{1,0:T(8,128)(2,1)}, bf16[1152,384]{1,0:T(8,128)(2,1)}, u32[]{:S(2)}, u32[]{:S(2)}) collective-permute-start(bf16[1152,384]{1,0:T(8,128)(2,1)} %get-tuple-element.59), channel_id=1, source_target_pairs={{0,4},{4,8},{8,12},{12,0},{1,5},{5,9},{9,13},{13,1},{2,6},{6,10},{... | collective-permute-start | bytes 2654216 | tf_op jit(solution)/shard_map/ppermute | solution.py:40
  393.3 34.8 %collective-permute-start.82 = (bf16[1152,384]{1,0:T(8,128)(2,1)}, bf16[1152,384]{1,0:T(8,128)(2,1)}, u32[]{:S(2)}, u32[]{:S(2)}) collective-permute-start(bf16[1152,384]{1,0:T(8,128)(2,1)} %get-tuple-element.58), channel_id=1, source_target_pairs={{0,8},{4,12},{8,0},{12,4},{1,9},{5,13},{9,1},{13,5},{2,10},{6,14},... | collective-permute-start | bytes 2654216 | tf_op jit(solution)/shard_map/ppermute | solution.py:40
  400.3 74.8 %collective-permute-start.63 = (bf16[4,1152,384]{2,1,0:T(8,128)(2,1)}, bf16[4,1152,384]{2,1,0:T(8,128)(2,1)}, u32[]{:S(2)}, u32[]{:S(2)}) collective-permute-start(bf16[4,1152,384]{2,1,0:T(8,128)(2,1)} %dynamic-slice_bitcast_fusion), channel_id=1, source_target_pairs={{0,1},{1,0},{2,3},{3,2},{4,5},{5,4},{6,7},{7,6},{8,9},{9,8},{10,11... | collective-permute-start | bytes 10616840 | tf_op jit(solution)/shard_map/ppermute | solution.py:40
  452.2 16.0 %collective-permute-start.90 = (bf16[8,144,384]{2,1,0:T(8,128)(2,1)S(1)}, bf16[8,144,384]{2,1,0:T(8,128)(2,1)S(1)}, u32[]{:S(2)}, u32[]{:S(2)}) collective-permute-start(bf16[8,144,384]{2,1,0:T(8,128)(2,1)S(1)} %constant_dynamic-update-slice_fusion.22), channel_id=1, source_target_pairs={{0,2},{2,0},{1,3},{3,1},{4,6},{6,4},{5,7},{7,5},{8,10},{10,8},{9,1... | collective-permute-start | bytes 2654216 | tf_op jit(solution)/shard_map/ppermute | solution.py:40
  468.4 19.3 %collective-permute-start.91 = (bf16[8,144,384]{2,1,0:T(8,128)(2,1)S(1)}, bf16[8,144,384]{2,1,0:T(8,128)(2,1)S(1)}, u32[]{:S(2)}, u32[]{:S(2)}) collective-permute-start(bf16[8,144,384]{2,1,0:T(8,128)(2,1)S(1)} %add_convert_fusion.1), channel_id=1, source_target_pairs={{0,4},{4,8},{8,12},{12,0},{1,5},{5,9},{9,13},{13,1},{2,6},{6,10},{... | collective-permute-start | bytes 2654216 | tf_op jit(solution)/shard_map/ppermute | solution.py:40
  471.3 21.2 %collective-permute-start.92 = (bf16[8,144,384]{2,1,0:T(8,128)(2,1)S(1)}, bf16[8,144,384]{2,1,0:T(8,128)(2,1)S(1)}, u32[]{:S(2)}, u32[]{:S(2)}) collective-permute-start(bf16[8,144,384]{2,1,0:T(8,128)(2,1)S(1)} %add_convert_fusion.1), channel_id=1, source_target_pairs={{0,12},{4,0},{8,4},{12,8},{1,13},{5,1},{9,5},{13,9},{2,14},{6,2},{... | collective-permute-start | bytes 2654216 | tf_op jit(solution)/shard_map/ppermute | solution.py:40
  473.4 34.8 %collective-permute-start.93 = (bf16[8,144,384]{2,1,0:T(8,128)(2,1)S(1)}, bf16[8,144,384]{2,1,0:T(8,128)(2,1)S(1)}, u32[]{:S(2)}, u32[]{:S(2)}) collective-permute-start(bf16[8,144,384]{2,1,0:T(8,128)(2,1)S(1)} %add_convert_fusion.1), channel_id=1, source_target_pairs={{0,8},{4,12},{8,0},{12,4},{1,9},{5,13},{9,1},{13,5},{2,10},{6,14},... | collective-permute-start | bytes 2654216 | tf_op jit(solution)/shard_map/ppermute | solution.py:40
  478.3 47.4 %collective-permute-start.64 = (bf16[1152,384]{1,0:T(8,128)(2,1)S(1)}, bf16[1152,384]{1,0:T(8,128)(2,1)S(1)}, u32[]{:S(2)}, u32[]{:S(2)}) collective-permute-start(bf16[1152,384]{1,0:T(8,128)(2,1)S(1)} %get-tuple-element.60), channel_id=1, source_target_pairs={{0,4},{4,8},{8,12},{12,0},{1,5},{5,9},{9,13},{13,1},{2,6},{6,10},{... | collective-permute-start | bytes 2654216 | tf_op jit(solution)/shard_map/ppermute | solution.py:40
  478.7 47.0 %collective-permute-start.65 = (bf16[1152,384]{1,0:T(8,128)(2,1)S(1)}, bf16[1152,384]{1,0:T(8,128)(2,1)S(1)}, u32[]{:S(2)}, u32[]{:S(2)}) collective-permute-start(bf16[1152,384]{1,0:T(8,128)(2,1)S(1)} %get-tuple-element.62), channel_id=1, source_target_pairs={{0,12},{4,0},{8,4},{12,8},{1,13},{5,1},{9,5},{13,9},{2,14},{6,2},{... | collective-permute-start | bytes 2654216 | tf_op jit(solution)/shard_map/ppermute | solution.py:40
  487.8 58.4 %collective-permute-start.66 = (bf16[1152,384]{1,0:T(8,128)(2,1)S(1)}, bf16[1152,384]{1,0:T(8,128)(2,1)S(1)}, u32[]{:S(2)}, u32[]{:S(2)}) collective-permute-start(bf16[1152,384]{1,0:T(8,128)(2,1)S(1)} %get-tuple-element.61), channel_id=1, source_target_pairs={{0,8},{4,12},{8,0},{12,4},{1,9},{5,13},{9,1},{13,5},{2,10},{6,14},... | collective-permute-start | bytes 2654216 | tf_op jit(solution)/shard_map/ppermute | solution.py:40
  508.9 104.6 %collective-permute-start.94 = (bf16[4,8,144,384]{3,2,1,0:T(8,128)(2,1)S(1)}, bf16[4,8,144,384]{3,2,1,0:T(8,128)(2,1)}, u32[]{:S(2)}, u32[]{:S(2)}) collective-permute-start(bf16[4,8,144,384]{3,2,1,0:T(8,128)(2,1)S(1)} %pad_maximum_fusion.3.mine_ref), channel_id=1, source_target_pairs={{0,1},{1,0},{2,3},{3,2},{4,5},{5,4},{6,7},{7,6},{8,9},{9,8},{10,11... | collective-permute-start | bytes 10616840 | tf_op jit(solution)/shard_map/ppermute | solution.py:40
  548.4 26.1 %collective-permute-start.67 = (bf16[144,384]{1,0:T(8,128)(2,1)S(1)}, bf16[144,384]{1,0:T(8,128)(2,1)}, u32[]{:S(2)}, u32[]{:S(2)}) collective-permute-start(bf16[144,384]{1,0:T(8,128)(2,1)S(1)} %get-tuple-element.89), channel_id=1, source_target_pairs={{0,32},{16,48},{32,64},{48,80},{64,96},{80,112},{96,0},{112,16},{1... | collective-permute-start | bytes 331784 | tf_op jit(solution)/shard_map/ppermute | solution.py:36
  548.4 31.1 %collective-permute-start.68 = (bf16[144,384]{1,0:T(8,128)(2,1)S(1)}, bf16[144,384]{1,0:T(8,128)(2,1)}, u32[]{:S(2)}, u32[]{:S(2)}) collective-permute-start(bf16[144,384]{1,0:T(8,128)(2,1)S(1)} %get-tuple-element.95), channel_id=1, source_target_pairs={{0,96},{16,112},{32,0},{48,16},{64,32},{80,48},{96,64},{112,80},{1... | collective-permute-start | bytes 331784 | tf_op jit(solution)/shard_map/ppermute | solution.py:36
  551.0 28.4 %collective-permute-start.69 = (bf16[144,384]{1,0:T(8,128)(2,1)S(1)}, bf16[144,384]{1,0:T(8,128)(2,1)}, u32[]{:S(2)}, u32[]{:S(2)}) collective-permute-start(bf16[144,384]{1,0:T(8,128)(2,1)S(1)} %get-tuple-element.94), channel_id=1, source_target_pairs={{0,16},{16,0},{32,48},{48,32},{64,80},{80,64},{96,112},{112,96},{1... | collective-permute-start | bytes 331784 | tf_op jit(solution)/shard_map/ppermute | solution.py:36
  (128 other events, 1316.7 us)

commit v2 on v1

--- a/solution.py
+++ b/solution.py
@@ -20,7 +20,6 @@
 GROUP = ("x", "yh")
 REPLICA = ("z", "yl", "core")
 SHIFTS = ((1, 0), (3, 0), (0, 1), (1, 1), (3, 1), (2, 0), (2, 1))
-Z_STEPS = (1, 3, 2)
 LANES = 128
 UNIT_TILES = 7
 
@@ -48,31 +47,28 @@
     return lax.dynamic_index_in_dim(stack, index, 0, keepdims=False)
 
 
-def place(stack, block, index):
-    return lax.dynamic_update_index_in_dim(stack, block, index, 0)
-
-
-def group_index(step=(0, 0), sign=1):
-    along_x = lax.rem(lax.axis_index("x") + 4 + sign * step[0], 4)
-    return along_x * 2 + (lax.axis_index("yh") ^ step[1])
-
-
-def gather_rows(shard):
-    stack = place(jnp.zeros((8,) + shard.shape, shard.dtype), shard, group_index())
-    for step in SHIFTS:
-        stack = place(stack, shifted(shard, step), group_index(step, -1))
-    return stack.reshape((-1,) + shard.shape[1:])
+def group_index():
+    return lax.axis_index("x") * 2 + lax.axis_index("yh")
+
+
+def exchanged(stack, axes):
+    return lax.all_to_all(stack, axes, 0, 0)
+
+
+def gathered(block, axes, size):
+    return exchanged(jnp.broadcast_to(block, (size,) + block.shape), axes)
+
+
+def on_first_core():
+    return lax.axis_index("core") == 0
 
 
 def by_core(first, second):
-    held = jnp.where(lax.axis_index("core") == 0, first, second)
-    return held
-
-
-def core_pair(held):
-    other = swapped(held, "core")
-    is_first = lax.axis_index("core") == 0
-    return jnp.where(is_first, held, other), jnp.where(is_first, other, held)
+    return jnp.where(on_first_core(), first, second)
+
+
+def both_cores(mine, other):
+    return by_core(mine, other), by_core(other, mine)
 
 
 def gather_tokens(rows):
@@ -90,13 +86,8 @@
 
 
 def piece_table():
-    depth, core = lax.axis_index("z"), lax.axis_index("core")
-    along = [lax.rem(depth + 4 - step, 4) for step in (0,) + Z_STEPS]
-    return jnp.stack([(core if own else 1 - core) * 4 + z for own in (True, False) for z in along])
-
-
-def source_table():
-    return jnp.stack([group_index(step, -1) for step in ((0, 0),) + SHIFTS])
+    core = lax.axis_index("core")
+    return jnp.stack([(core if own else 1 - core) * 4 + z for own in (True, False) for z in range(4)])
 
 
 def unit_kernel(piece_ref, gate_ref, up_ref, down_ref, out_ref):
@@ -128,15 +119,10 @@
 
 
 def unit_shards(pieces):
-    me = group_index()
-    stack = place(jnp.zeros_like(pieces), pick(pieces, me), me)
-    for step in SHIFTS:
-        block = shifted(pick(pieces, group_index(step)), step)
-        stack = place(stack, block, group_index(step, -1))
-    stack = stack.reshape(-1, 3 * LANES)
-    mine = [stack] + [turned(stack, "z", step, 4) for step in Z_STEPS]
-    other = swapped(jnp.stack(mine), "core")
-    slots = mine + [other[i] for i in range(4)]
+    stack = exchanged(pieces, GROUP).reshape(-1, 3 * LANES)
+    mine = gathered(stack, "z", 4)
+    other = swapped(mine, "core")
+    slots = [mine[i] for i in range(4)] + [other[i] for i in range(4)]
     return tuple(
         jnp.concatenate([slot[:, i * LANES : (i + 1) * LANES] for slot in slots], axis=1)
         for i in range(3)
@@ -145,6 +131,10 @@
 
 def plus(*blocks):
     return sum(block.astype(jnp.float32) for block in blocks).astype(jnp.bfloat16)
+
+
+def summed(stack):
+    return jnp.sum(stack.astype(jnp.float32), axis=0).astype(jnp.bfloat16)
 
 
 def assemble_units_kernel(table_ref, mine_ref, other_ref, *out_refs):
@@ -162,7 +152,7 @@
 
 def assemble_units(mine, other, units):
     rows = mine.shape[2]
-    table = jnp.concatenate([piece_table(), source_table()])
+    table = piece_table()
     block = UNIT_TILES * LANES
     spec = pl.BlockSpec((4, 1, rows, 3 * LANES), lambda r, table: (0, r, 0, 0))
     return pl.pallas_call(
@@ -172,7 +162,7 @@
             num_scalar_prefetch=1,
             grid=(8,),
             in_specs=[spec] * 2,
-            out_specs=[pl.BlockSpec((rows, block), lambda r, table: (0, table[8 + r]))] * 3,
+            out_specs=[pl.BlockSpec((rows, block), lambda r, table: (0, r))] * 3,
         ),
         compiler_params=pltpu.CompilerParams(vmem_limit_bytes=32 * 2**20),
     )(table, mine, other)
@@ -210,41 +200,35 @@
     return jnp.transpose(grad.reshape(grad.shape[0], -1, LANES), (1, 0, 2))
 
 
-def unit_grads(grad_gate, grad_up, grad_down, units):
-    slots = jnp.concatenate([to_slots(g) for g in (grad_gate, grad_up, grad_down)], axis=2)
-    mine, other = slots[:4], slots[4:]
-    total = plus(mine, swapped(other, "core"))
-    total = plus(
-        total[0],
-        *[turned(total[1 + i], "z", (4 - step) % 4, 4) for i, step in enumerate(Z_STEPS)],
-    )
-    total = total.reshape(8, 144, 3 * LANES)
-    blocks = [pick(total, group_index())]
-    blocks += [shifted(pick(total, group_index(step)), step) for step in SHIFTS]
-    stack = jnp.stack(blocks)
+def unit_slots(*grads):
+    return jnp.concatenate([to_slots(g) for g in grads], axis=2)
+
+
+def unit_part(slots):
+    return summed(exchanged(plus(slots[:4], swapped(slots[4:], "core")), "z"))
+
+
+def unit_grads(parts, units):
+    total = jnp.concatenate(parts, axis=1).reshape(8, 144, 3 * LANES)
+    stack = exchanged(total, GROUP)
     stack = plus(stack, swapped(stack, "yl"))
-    mine = jnp.stack([stack] + [turned(stack, "z", step, 4) for step in Z_STEPS])
+    mine = gathered(stack, "z", 4)
     return assemble_units(mine, swapped(mine, "core"), units)
 
 
-def attn_grads_of(grad_projected, grad_out):
-    query, pair = grad_projected[:, :1024], grad_projected[:, 1024:]
-    pair = jnp.pad(pair, ((0, 0), (0, 512)))
-    slots = jnp.concatenate([to_slots(g) for g in (query, grad_out, pair)], axis=2)
-    core, depth = lax.axis_index("core"), lax.axis_index("z")
+def attn_part(*grads):
+    slots = jnp.concatenate([to_slots(g) for g in grads], axis=2)
     halves = slots.reshape((2, 4) + slots.shape[1:])
+    core = lax.axis_index("core")
     total = plus(pick(halves, core), swapped(pick(halves, 1 - core), "core"))
-    total = plus(
-        pick(total, depth),
-        *[turned(pick(total, lax.rem(depth + step, 4)), "z", step, 4) for step in Z_STEPS],
-    )
-    total = total.reshape(8, 144, 3 * LANES)
-    total = plus(
-        pick(total, group_index()),
-        *[shifted(pick(total, group_index(step)), step) for step in SHIFTS],
-    )
+    return summed(exchanged(total, "z"))
+
+
+def attn_grads_of(query_pair, out):
+    total = jnp.concatenate([query_pair[:, :LANES], out, query_pair[:, LANES:]], axis=1)
+    total = summed(exchanged(total.reshape(8, 144, 3 * LANES), GROUP))
     total = plus(total, swapped(total, "yl"))
-    mine = jnp.stack([total] + [turned(total, "z", step, 4) for step in Z_STEPS])
+    mine = gathered(total, "z", 4)
     return assemble_attn(mine, swapped(mine, "core"))
 
 
@@ -346,17 +330,18 @@
     qkv_held = by_core(
         w_query[:, :768], jnp.concatenate([w_query[:, 768:], w_key, w_value], axis=1)
     )
-    qkv_rows = lax.all_to_all(jnp.broadcast_to(qkv_held, (8,) + qkv_held.shape), GROUP, 0, 0)
     unit_held = unit_pieces(w_gate, w_up, w_down)
-    qkv_first, qkv_second = core_pair(qkv_rows.reshape(model_width, -1))
+    qkv_mine = gathered(qkv_held, GROUP, 8).reshape(model_width, -1)
+    qkv_other = swapped(qkv_mine, "core")
     out_held = by_core(w_out[:, :512], w_out[:, 512:])
-    out_held, unit_held, _ = lax.optimization_barrier((out_held, unit_held, qkv_rows))
-    out_rows = gather_rows(out_held)
-    out_first, out_second = core_pair(out_rows)
-    unit_held, _ = lax.optimization_barrier((unit_held, out_rows))
+    out_held, unit_held, _ = lax.optimization_barrier((out_held, unit_held, qkv_other))
+    out_mine = gathered(out_held, GROUP, 8).reshape(model_width, -1)
+    out_other = swapped(out_mine, "core")
     gate_cols, up_cols, down_cols = unit_shards(unit_held)
-    first_raw = jnp.dot(normed, qkv_first, preferred_element_type=jnp.float32)
-    second_raw = jnp.dot(normed, qkv_second, preferred_element_type=jnp.float32)
+    first_raw, second_raw = both_cores(
+        jnp.dot(normed, qkv_mine, preferred_element_type=jnp.float32),
+        jnp.dot(normed, qkv_other, preferred_element_type=jnp.float32),
+    )
     query_raw = jnp.concatenate([first_raw, second_raw[:, :256]], axis=1)
     key_raw = second_raw[:, 256:512]
     value_raw = second_raw[:, 512:]
@@ -400,8 +385,9 @@
         "shqk,skd->sqhd", weights, value_rows, preferred_element_type=jnp.float32
     )
     attended = mixed_heads.reshape(all_rows, query_cols).astype(jnp.bfloat16)
-    attn_branch = product_by_rows(attended[:, :512], out_first) + product_by_rows(
-        attended[:, 512:], out_second
+    attended_mine, attended_other = both_cores(attended[:, :512], attended[:, 512:])
+    attn_branch = product_by_rows(attended_mine, out_mine) + product_by_rows(
+        attended_other, out_other
     )
     attn_normed, norm_post_attn_back = jax.vjp(norm_rows, attn_branch, gain_post_attn)
     middle = inputs + attn_normed
@@ -423,24 +409,37 @@
     grad_gate_full, grad_up_full = gelu_back(grad_hidden)
     grad_gate_part = grad_gate_full.astype(jnp.bfloat16)
     grad_up_part = grad_up_full.astype(jnp.bfloat16)
-    grad_normed_ffn = scatter_tokens(
-        product_by_rows(grad_gate_part, gate_cols) + product_by_rows(grad_up_part, up_cols)
+    grad_partial = product_by_rows(grad_gate_part, gate_cols) + product_by_rows(
+        grad_up_part, up_cols
+    )
+    grad_normed_ffn = scatter_tokens(grad_partial)
+    ffn_rows, grad_branch_rows, _ = lax.optimization_barrier(
+        (ffn_rows, grad_branch_rows, grad_partial)
+    )
+    down_part = unit_part(
+        unit_slots(transposed_product(grad_branch_rows, hidden).astype(jnp.bfloat16))
+    )
+    gate_up_part = unit_part(
+        unit_slots(
+            transposed_product(ffn_rows, grad_gate_part).astype(jnp.bfloat16),
+            transposed_product(ffn_rows, grad_up_part).astype(jnp.bfloat16),
+        )
     )
     grad_gate_total, grad_up_total, grad_down_total = unit_grads(
-        transposed_product(ffn_rows, grad_gate_part).astype(jnp.bfloat16),
-        transposed_product(ffn_rows, grad_up_part).astype(jnp.bfloat16),
-        transposed_product(grad_branch_rows, hidden).astype(jnp.bfloat16),
-        w_gate.shape[1],
+        (gate_up_part, down_part), w_gate.shape[1]
     )
     grad_middle_part, grad_gain_ffn = norm_ffn_back(grad_normed_ffn)
     grad_middle = upstream + grad_middle_part
     grad_attn_branch, grad_post_attn = norm_post_attn_back(grad_middle)
     grad_attn_branch = grad_attn_branch.astype(jnp.bfloat16)
+    out_part = attn_part(
+        transposed_product(grad_attn_branch, attended).astype(jnp.bfloat16)
+    )
     grad_attended = jnp.concatenate(
-        [
-            jnp.dot(grad_attn_branch, out_first, preferred_element_type=jnp.float32),
-            jnp.dot(grad_attn_branch, out_second, preferred_element_type=jnp.float32),
-        ],
+        both_cores(
+            jnp.dot(grad_attn_branch, out_mine, preferred_element_type=jnp.float32),
+            jnp.dot(grad_attn_branch, out_other, preferred_element_type=jnp.float32),
+        ),
         axis=1,
     )
     grad_heads = grad_attended.astype(jnp.bfloat16).reshape(seq_count, tok_rows, HEADS, head_width)
@@ -477,12 +476,17 @@
     grad_projected = jnp.concatenate([grad_query_raw, grad_key_raw, grad_value_raw], axis=1).astype(
         jnp.bfloat16
     )
-    contribution = product_by_rows(grad_projected[:, :768], qkv_first) + product_by_rows(
-        grad_projected[:, 768:], qkv_second
-    )
+    projected_mine, projected_other = both_cores(grad_projected[:, :768], grad_projected[:, 768:])
+    contribution = product_by_rows(projected_mine, qkv_mine) + product_by_rows(
+        projected_other, qkv_other
+    )
+    projected_part = transposed_product(normed, grad_projected).astype(jnp.bfloat16)
     query_total, grad_out_total, pair_total = attn_grads_of(
-        transposed_product(normed, grad_projected).astype(jnp.bfloat16),
-        transposed_product(grad_attn_branch, attended).astype(jnp.bfloat16),
+        attn_part(
+            projected_part[:, :query_cols],
+            jnp.pad(projected_part[:, query_cols:], ((0, 0), (0, 512))),
+        ),
+        out_part,
     )
     grad_inputs_part, grad_gain_attn = norm_attn_back(contribution)
     grad_tokens = (grad_middle + grad_inputs_part).reshape(seq_count, tok_rows, model_width)

time: 632 us -> 608 us (0.962)
  starting transfers between devices: 230 us -> 185 us
  other arithmetic: 37 us -> 55.3 us
    all_to_all x1 -> x12, waiting for transfers between devices: 18.7 us -> 139 us  [exchanged(): return lax.all_to_all(stack, axes, 0, 0)]
    ppermute x27 -> x14, waiting for transfers between devices: 113 us -> 5.34 us  [turned(): lax.ppermute(block, axis, [(i, (i + step) % size) for i in range(size)])]
    ppermute x56 -> x28, starting transfers between devices: 116 us -> 50.7 us  [shifted(): return lax.ppermute(block, GROUP, route)]
    all_to_all x1 -> x12, starting transfers between devices: 7.48 us -> 71.6 us  [exchanged(): return lax.all_to_all(stack, axes, 0, 0)]
    ppermute x27 -> x14, starting transfers between devices: 84 us -> 40.7 us  [turned(): lax.ppermute(block, axis, [(i, (i + step) % size) for i in range(size)])]
    reshape x5 -> x0, local copies, waits for them, and re-layouts: 17.4 us -> none  [the longest x4 17.3 us: to_slots(): return jnp.transpose(grad.reshape(grad.shape[0], -1, LANES), (1, 0, 2))]
    unnamed x198 -> x173, local copies, waits for them, and re-layouts: 23.2 us -> 34.4 us
    reduce_sum x0 -> x5, other arithmetic: none -> 10.9 us  [summed(): return jnp.sum(stack.astype(jnp.float32), axis=0).astype(jnp.bfloat16)]
  transfers between devices with their start and end apart: 96 -> 66, of which waited for: 39 -> 27; matrix products, arithmetic and copies ran while one was open for 17% -> 21% of each run, Pallas kernels for 1% -> 1%
where the time goes in v2:
time: 608 us; the launch traced here: 597 us
  waiting for transfers between devices  207 us (34%)
  starting transfers between devices  185 us (30%)
  matrix products  66 us (11%)
  local copies, waits for them, and re-layouts  64.5 us (11%)
  other arithmetic  55.3 us (9%)
  Pallas kernels  16.4 us (3%)
    all_to_all x12, waiting for transfers between devices, exchanged(): return lax.all_to_all(stack, axes, 0, 0)  139 us
    all_to_all x12, starting transfers between devices, exchanged(): return lax.all_to_all(stack, axes, 0, 0)  71.6 us
    ppermute x28, waiting for transfers between devices, shifted(): return lax.ppermute(block, GROUP, route)  56.8 us
    ppermute x28, starting transfers between devices, shifted(): return lax.ppermute(block, GROUP, route)  50.7 us
    ppermute x14, starting transfers between devices, turned(): lax.ppermute(block, axis, [(i, (i + step) % size) for i in range(size)])  40.7 us
    unnamed x173, local copies, waits for them, and re-layouts  34.4 us
    ppermute x8, starting transfers between devices, from_behind(): return lax.ppermute(block, GROUP, route)  17.1 us
    dot_general x7, matrix products, product_by_rows(): lax.dot_general(left_side, right_side, CONTRACT_COLS, preferred_element_t...  17 us
  transfers between devices with their start and end apart: 66, of which 27 were waited for; matrix products, arithmetic and copies ran while one was open for 21% of the time, Pallas kernels for 1%

profile of v2, /device:TPU:1, one launch (start us, length us, event | category | flops | bytes accessed | tf_op | source)
XLA Modules:
  0.0 596.9 jit_solution(8874786854748741627)
XLA Ops:
  3.9 7.5 %all-to-all-start = ((bf16[8,144,768]{2,1,0:T(8,128)(2,1)}), bf16[8,144,768]{2,1,0:T(8,128)(2,1)S(1)}, u32[]{:S(2)}, u32[]{:S(2)}) async-start(bf16[8,144,768]{2,1,0:T(8,128)(2,1)} %broadcast_in_dim.38), calls=%async_computation | async-start | bytes 3538944 | tf_op jit(solution)/shard_map/all_to_all | solution.py:55
  12.0 5.6 shard_map.271
  17.7 19.5 %all-to-all-done = bf16[8,144,768]{2,1,0:T(8,128)(2,1)S(1)} async-done(((bf16[8,144,768]{2,1,0:T(8,128)(2,1)}), bf16[8,144,768]{2,1,0:T(8,128)(2,1)S(1)}, u32[]{:S(2)}, u32[]{:S(2)}) %all-to-all-start) | async-done | bytes 1769504 | tf_op jit(solution)/shard_map/all_to_all | solution.py:55
  47.3 4.0 collective-permute-start.2
  57.9 4.3 all-to-all-start.1
  66.3 12.7 %all-to-all-done.1 = bf16[8,144,512]{2,1,0:T(8,128)(2,1)} async-done(((bf16[8,144,512]{2,1,0:T(8,128)(2,1)}), bf16[8,144,512]{2,1,0:T(8,128)(2,1)}, u32[]{:S(2)}, u32[]{:S(2)}) %all-to-all-start.1) | async-done | bytes 1179680 | tf_op jit(solution)/shard_map/all_to_all | solution.py:55
  79.0 4.0 all-to-all-start.2
  87.3 9.4 %all-to-all-done.2 = bf16[8,144,384]{2,1,0:T(8,128)(2,1)S(1)} async-done(((bf16[8,144,384]{2,1,0:T(8,128)(2,1)}), bf16[8,144,384]{2,1,0:T(8,128)(2,1)S(1)}, u32[]{:S(2)}, u32[]{:S(2)}) %all-to-all-start.2) | async-done | bytes 884768 | tf_op jit(solution)/shard_map/all_to_all | solution.py:55
  98.9 5.0 all-to-all-start.3
  113.0 4.6 collective-permute-start.10
  118.3 4.7 collective-permute-start.12
  123.7 8.8 %collective-permute-done.8 = bf16[128,1152]{1,0:T(8,128)(2,1)S(1)} collective-permute-done((bf16[128,1152]{1,0:T(8,128)(2,1)}, bf16[128,1152]{1,0:T(8,128)(2,1)S(1)}, u32[]{:S(2)}, u32[]{:S(2)}) %collective-permute-start.8) | collective-permute-done | bytes 294944 | tf_op jit(solution)/shard_map/ppermute | solution.py:35
  133.3 11.4 %all-to-all-done.3 = bf16[4,1152,384]{2,1,0:T(8,128)(2,1)} async-done(((bf16[4,1152,384]{2,1,0:T(8,128)(2,1)}), bf16[4,1152,384]{2,1,0:T(8,128)(2,1)}, u32[]{:S(2)}, u32[]{:S(2)}) %all-to-all-start.3) | async-done | bytes 3538976 | tf_op jit(solution)/shard_map/all_to_all | solution.py:55
  159.1 6.3 %fusion.141 = f32[1024,1024]{1,0:T(8,128)S(1)} fusion(bf16[1024,1152]{1,0:T(8,128)(2,1)} %constant_dynamic-update-slice_fusion.5, bf16[1152,1024]{1,0:T(8,128)(2,1)S(1)} %get-tuple-element.83), kind=kOutput, calls=%fused_computation.311 | convolution fusion | flops 2415919104 | bytes 8912896 | tf_op jit(solution)/shard_map/dot_general | solution.py:397
  165.4 8.3 %multiply_convert_fusion.1 = (bf16[1024,1024]{1,0:T(8,128)(2,1)S(1)}, f32[1024,1024]{1,0:T(8,128)}) fusion(f32[1024,1024]{1,0:T(8,128)S(1)} %fusion.141, bf16[1024,1152]{1,0:T(8,128)(2,1)} %constant_dynamic-update-slice_fusion.5, bf16[1152,1024]{1,0:T(8,128)(2,1)S(1)} %get-tuple-element.82), kind=kOutput, calls=%fused_computation.18 | convolution fusion | flops 2426404864 | bytes 15204352 | tf_op jit(solution)/shard_map/dot_general | solution.py:398
  189.2 11.3 %collective-permute-done.16 = bf16[128,1152]{1,0:T(8,128)(2,1)S(1)} collective-permute-done((bf16[128,1152]{1,0:T(8,128)(2,1)S(1)}, bf16[128,1152]{1,0:T(8,128)(2,1)S(1)}, u32[]{:S(2)}, u32[]{:S(2)}) %collective-permute-start.16) | collective-permute-done | bytes 294944 | tf_op jit(solution)/shard_map/ppermute | solution.py:35
  203.9 8.7 %collective-permute-done.20 = bf16[128,1152]{1,0:T(8,128)(2,1)S(1)} collective-permute-done((bf16[128,1152]{1,0:T(8,128)(2,1)S(1)}, bf16[128,1152]{1,0:T(8,128)(2,1)S(1)}, u32[]{:S(2)}, u32[]{:S(2)}) %collective-permute-start.20) | collective-permute-done | bytes 294944 | tf_op jit(solution)/shard_map/ppermute | solution.py:35
  220.2 3.8 collective-permute-start.25
  226.5 4.5 collective-permute-start.27
  231.8 8.4 %collective-permute-done.23 = bf16[128,1152]{1,0:T(8,128)(2,1)S(1)} collective-permute-done((bf16[128,1152]{1,0:T(8,128)(2,1)}, bf16[128,1152]{1,0:T(8,128)(2,1)S(1)}, u32[]{:S(2)}, u32[]{:S(2)}) %collective-permute-start.23) | collective-permute-done | bytes 294944 | tf_op jit(solution)/shard_map/ppermute | solution.py:35
  245.6 8.8 %fusion.7 = (bf16[1024,1024]{1,0:T(8,128)(2,1)S(1)}, bf16[1024,1024]{1,0:T(8,128)(2,1)S(1)}) fusion(f32[1024,1024]{1,0:T(8,128)} %copy-done.66, f32[1024,1024]{1,0:T(8,128)} %get-tuple-element.145, bf16[1024,1152]{1,0:T(8,128)(2,1)} %constant_dynamic-update-slice_fusion.13, bf16[1152,1024]{1,0:T(8,128)(2,1)S(1)} %copy-done.44), kind=kOutput, calls=%fused_computation.16 | convolution fusion | flops 2441084928 | bytes 17301504 | tf_op jit(solution)/shard_map/dot_general | solution.py:408
  260.4 4.9 convolution_convert_fusion.4
  265.3 5.8 convolution_convert_fusion.3
  271.3 4.6 collective-permute-start.28
  292.1 7.1 %collective-permute-done.30 = bf16[128,1152]{1,0:T(8,128)(2,1)S(1)} collective-permute-done((bf16[128,1152]{1,0:T(8,128)(2,1)S(1)}, bf16[128,1152]{1,0:T(8,128)(2,1)S(1)}, u32[]{:S(2)}, u32[]{:S(2)}) %collective-permute-start.30) | collective-permute-done | bytes 294944 | tf_op jit(solution)/shard_map/ppermute | solution.py:35
  299.2 5.8 collective-permute-start.50
  305.0 3.7 collective-permute-done.34
  332.5 4.3 all-to-all-start.9
  338.2 4.3 add_convert_fusion
  342.5 11.0 %all-to-all-done.9 = bf16[4,1152,128]{1,2,0:T(8,128)(2,1)} async-done(((bf16[4,1152,128]{1,2,0:T(8,128)(2,1)}), bf16[4,1152,128]{1,2,0:T(8,128)(2,1)}, u32[]{:S(2)}, u32[]{:S(2)}) %all-to-all-start.9) | async-done | bytes 1179680 | tf_op jit(solution)/shard_map/all_to_all | solution.py:55
  353.5 4.7 all-to-all-start.8
  361.9 24.8 %all-to-all-done.8 = bf16[4,1152,256]{1,2,0:T(8,128)(2,1)} async-done(((bf16[4,1152,256]{1,2,0:T(8,128)(2,1)}), bf16[4,1152,256]{1,2,0:T(8,128)(2,1)}, u32[]{:S(2)}, u32[]{:S(2)}) %all-to-all-start.8) | async-done | bytes 2359328 | tf_op jit(solution)/shard_map/all_to_all | solution.py:55
  390.4 9.9 %all-to-all-start.10 = ((bf16[8,144,384]{2,1,0:T(8,128)(2,1)}), bf16[8,144,384]{2,1,0:T(8,128)(2,1)}, u32[]{:S(2)}, u32[]{:S(2)}) async-start(bf16[8,144,384]{2,1,0:T(8,128)(2,1)} %bitcast.81), calls=%async_computation.10 | async-start | bytes 1769472 | tf_op jit(solution)/shard_map/all_to_all | solution.py:55
  407.2 4.5 all-to-all-done.10
  414.8 3.7 all-to-all-start.5
  424.4 4.6 collective-permute-start.46
  432.9 4.5 all-to-all-start.11
  437.3 4.3 fusion
  441.7 33.1 %all-to-all-done.11.mine_ref = bf16[4,8,144,384]{3,2,1,0:T(8,128)(2,1)S(1)} async-done(((bf16[4,8,144,384]{3,2,1,0:T(8,128)(2,1)}), bf16[4,8,144,384]{3,2,1,0:T(8,128)(2,1)S(1)}, u32[]{:S(2)}, u32[]{:S(2)}) %all-to-all-start.11) | async-done | bytes 3538976 | tf_op jit(solution)/shard_map/all_to_all | solution.py:55
  474.8 4.5 all-to-all-start.4
  479.4 5.7 collective-permute-start.53
  493.7 9.5 %all-to-all-done.4 = bf16[4,1152,256]{2,1,0:T(8,128)(2,1)} async-done(((bf16[4,1152,256]{2,1,0:T(8,128)(2,1)}), bf16[4,1152,256]{2,1,0:T(8,128)(2,1)}, u32[]{:S(2)}, u32[]{:S(2)}) %all-to-all-start.4) | async-done | bytes 2359328 | tf_op jit(solution)/shard_map/all_to_all | solution.py:55
  509.3 15.2 %all-to-all-start.6 = ((bf16[8,144,384]{2,1,0:T(8,128)(2,1)}), bf16[8,144,384]{2,1,0:T(8,128)(2,1)}, u32[]{:S(2)}, u32[]{:S(2)}) async-start(bf16[8,144,384]{2,1,0:T(8,128)(2,1)} %bitcast.249), calls=%async_computation.6 | async-start | bytes 1769472 | tf_op jit(solution)/shard_map/all_to_all | solution.py:55
  532.3 3.8 collective-permute-start.39
  548.9 3.8 collective-permute-done.43
  564.5 4.1 all-to-all-start.7
  575.2 6.9 %collective-permute-start.49 = (bf16[4,144,384]{2,1,0:T(8,128)(2,1)}, bf16[4,144,384]{2,1,0:T(8,128)(2,1)S(1)}, u32[]{:S(2)}, u32[]{:S(2)}) collective-permute-start(bf16[4,144,384]{2,1,0:T(8,128)(2,1)} %all-to-all-done.7.mine_ref), channel_id=1, source_target_pairs={{0,1},{1,0},{2,3},{3,2},{4,5},{5,4},{6,7},{7,6},{8,9},{9,8},{10,11... | collective-permute-start | bytes 1327112 | tf_op jit(solution)/shard_map/ppermute | solution.py:39
  587.9 8.5 %shard_map.273 = (f32[144,6912]{1,0:T(8,128)}, f32[144,6912]{1,0:T(8,128)}, f32[144,6912]{1,0:T(8,128)}) custom-call(s32[8]{0:T(128)S(1)} %stack.52.table_ref, bf16[4,8,144,384]{3,2,1,0:T(8,128)(2,1)S(1)} %all-to-all-done.11.mine_ref, bf16[4,8,144,384]{3,2,1,0:T(8,128)(2,1)} %collective-permute-done.53.other_ref), custom_call_target="tpu_custom_call" | custom-call | tf_op jit(solution)/shard_map/pallas_call | solution.py:158
  (395 shorter events, 224.8 us)
Async XLA Ops:
  3.9 33.2 %all-to-all-start = ((bf16[8,144,768]{2,1,0:T(8,128)(2,1)}), bf16[8,144,768]{2,1,0:T(8,128)(2,1)S(1)}, u32[]{:S(2)}, u32[]{:S(2)}) async-start(bf16[8,144,768]{2,1,0:T(8,128)(2,1)} %broadcast_in_dim.38), calls=%async_computation | async-start | bytes 3538944 | tf_op jit(solution)/shard_map/all_to_all | solution.py:55
  44.4 18.0 %collective-permute-start.1 = (bf16[1,128,512]{2,1,0:T(8,128)(2,1)}, bf16[1,128,512]{2,1,0:T(8,128)(2,1)}, u32[]{:S(2)}, u32[]{:S(2)}) collective-permute-start(bf16[1,128,512]{2,1,0:T(8,128)(2,1)} %pad_maximum_fusion.8), channel_id=1, source_target_pairs={{0,64},{16,80},{32,96},{48,112},{1,65},{17,81},{33,97},{49,113},{2... | collective-permute-start | bytes 393224 | tf_op jit(solution)/shard_map/ppermute | solution.py:30
  47.3 16.2 %collective-permute-start.2 = (bf16[1,128,512]{2,1,0:T(8,128)(2,1)}, bf16[1,128,512]{2,1,0:T(8,128)(2,1)}, u32[]{:S(2)}, u32[]{:S(2)}) collective-permute-start(bf16[1,128,512]{2,1,0:T(8,128)(2,1)} %pad_maximum_fusion.8), channel_id=1, source_target_pairs={{0,48},{16,64},{32,80},{48,96},{64,112},{1,49},{17,65},{33,81},{49... | collective-permute-start | bytes 393224 | tf_op jit(solution)/shard_map/ppermute | solution.py:30
  51.4 13.1 %collective-permute-start.3 = (bf16[1,128,512]{2,1,0:T(8,128)(2,1)}, bf16[1,128,512]{2,1,0:T(8,128)(2,1)}, u32[]{:S(2)}, u32[]{:S(2)}) collective-permute-start(bf16[1,128,512]{2,1,0:T(8,128)(2,1)} %pad_maximum_fusion.8), channel_id=1, source_target_pairs={{0,32},{16,48},{32,64},{48,80},{64,96},{80,112},{1,33},{17,49},{33... | collective-permute-start | bytes 393224 | tf_op jit(solution)/shard_map/ppermute | solution.py:30
  53.3 12.1 %collective-permute-start.4 = (bf16[1,128,512]{2,1,0:T(8,128)(2,1)}, bf16[1,128,512]{2,1,0:T(8,128)(2,1)}, u32[]{:S(2)}, u32[]{:S(2)}) collective-permute-start(bf16[1,128,512]{2,1,0:T(8,128)(2,1)} %pad_maximum_fusion.8), channel_id=1, source_target_pairs={{0,16},{16,32},{32,48},{48,64},{64,80},{80,96},{96,112},{1,17},{17... | collective-permute-start | bytes 393224 | tf_op jit(solution)/shard_map/ppermute | solution.py:30
  57.9 21.1 %all-to-all-start.1 = ((bf16[8,144,512]{2,1,0:T(8,128)(2,1)}), bf16[8,144,512]{2,1,0:T(8,128)(2,1)}, u32[]{:S(2)}, u32[]{:S(2)}) async-start(bf16[8,144,512]{2,1,0:T(8,128)(2,1)} %broadcast_in_dim.41), calls=%async_computation.1 | async-start | bytes 2359296 | tf_op jit(solution)/shard_map/all_to_all | solution.py:55
  79.0 17.8 %all-to-all-start.2 = ((bf16[8,144,384]{2,1,0:T(8,128)(2,1)}), bf16[8,144,384]{2,1,0:T(8,128)(2,1)S(1)}, u32[]{:S(2)}, u32[]{:S(2)}) async-start(bf16[8,144,384]{2,1,0:T(8,128)(2,1)} %shard_map.271), calls=%async_computation.2 | async-start | bytes 1769472 | tf_op jit(solution)/shard_map/all_to_all | solution.py:55
  83.0 22.7 %collective-permute-start.5 = (bf16[1152,512]{1,0:T(8,128)(2,1)}, bf16[1152,512]{1,0:T(8,128)(2,1)}, u32[]{:S(2)}, u32[]{:S(2)}) collective-permute-start(bf16[1152,512]{1,0:T(8,128)(2,1)} %bitcast.19), channel_id=1, source_target_pairs={{0,1},{1,0},{2,3},{3,2},{4,5},{5,4},{6,7},{7,6},{8,9},{9,8},{10,11... | collective-permute-start | bytes 3538952 | tf_op jit(solution)/shard_map/ppermute | solution.py:39
  98.9 45.8 %all-to-all-start.3 = ((bf16[4,1152,384]{2,1,0:T(8,128)(2,1)}), bf16[4,1152,384]{2,1,0:T(8,128)(2,1)}, u32[]{:S(2)}, u32[]{:S(2)}) async-start(bf16[4,1152,384]{2,1,0:T(8,128)(2,1)} %broadcast_in_dim.42), calls=%async_computation.3 | async-start | bytes 7077888 | tf_op jit(solution)/shard_map/all_to_all | solution.py:55
  111.5 21.1 %collective-permute-start.8 = (bf16[128,1152]{1,0:T(8,128)(2,1)}, bf16[128,1152]{1,0:T(8,128)(2,1)S(1)}, u32[]{:S(2)}, u32[]{:S(2)}) collective-permute-start(bf16[128,1152]{1,0:T(8,128)(2,1)} %get-tuple-element.54), channel_id=1, source_target_pairs={{0,16},{16,0},{32,48},{48,32},{64,80},{80,64},{96,112},{112,96},{1... | collective-permute-start | bytes 884744 | tf_op jit(solution)/shard_map/ppermute | solution.py:35
  112.5 34.9 %collective-permute-start.9 = (bf16[128,1152]{1,0:T(8,128)(2,1)}, bf16[128,1152]{1,0:T(8,128)(2,1)}, u32[]{:S(2)}, u32[]{:S(2)}) collective-permute-start(bf16[128,1152]{1,0:T(8,128)(2,1)} %get-tuple-element.54), channel_id=1, source_target_pairs={{0,48},{16,32},{32,80},{48,64},{64,112},{80,96},{96,16},{112,0},{1... | collective-permute-start | bytes 884744 | tf_op jit(solution)/shard_map/ppermute | solution.py:35
  113.0 36.1 %collective-permute-start.10 = (bf16[128,1152]{1,0:T(8,128)(2,1)}, bf16[128,1152]{1,0:T(8,128)(2,1)S(1)}, u32[]{:S(2)}, u32[]{:S(2)}) collective-permute-start(bf16[128,1152]{1,0:T(8,128)(2,1)} %get-tuple-element.54), channel_id=1, source_target_pairs={{0,112},{16,96},{32,16},{48,0},{64,48},{80,32},{96,80},{112,64},{1... | collective-permute-start | bytes 884744 | tf_op jit(solution)/shard_map/ppermute | solution.py:35
  117.6 32.2 %collective-permute-start.11 = (bf16[128,1152]{1,0:T(8,128)(2,1)}, bf16[128,1152]{1,0:T(8,128)(2,1)}, u32[]{:S(2)}, u32[]{:S(2)}) collective-permute-start(bf16[128,1152]{1,0:T(8,128)(2,1)} %get-tuple-element.54), channel_id=1, source_target_pairs={{0,64},{16,80},{32,96},{48,112},{64,0},{80,16},{96,32},{112,48},{1... | collective-permute-start | bytes 884744 | tf_op jit(solution)/shard_map/ppermute | solution.py:35
  118.3 33.2 %collective-permute-start.12 = (bf16[128,1152]{1,0:T(8,128)(2,1)}, bf16[128,1152]{1,0:T(8,128)(2,1)}, u32[]{:S(2)}, u32[]{:S(2)}) collective-permute-start(bf16[128,1152]{1,0:T(8,128)(2,1)} %get-tuple-element.54), channel_id=1, source_target_pairs={{0,80},{16,64},{32,112},{48,96},{64,16},{80,0},{96,48},{112,32},{1... | collective-permute-start | bytes 884744 | tf_op jit(solution)/shard_map/ppermute | solution.py:35
  144.7 12.3 %collective-permute-start.13 = (bf16[4,1152,384]{2,1,0:T(8,128)(2,1)}, bf16[4,1152,384]{2,1,0:T(8,128)(2,1)S(1)}, u32[]{:S(2)}, u32[]{:S(2)}) collective-permute-start(bf16[4,1152,384]{2,1,0:T(8,128)(2,1)} %all-to-all-done.3), channel_id=1, source_target_pairs={{0,1},{1,0},{2,3},{3,2},{4,5},{5,4},{6,7},{7,6},{8,9},{9,8},{10,11... | collective-permute-start | bytes 10616840 | tf_op jit(solution)/shard_map/ppermute | solution.py:39
  178.4 22.1 %collective-permute-start.16 = (bf16[128,1152]{1,0:T(8,128)(2,1)S(1)}, bf16[128,1152]{1,0:T(8,128)(2,1)S(1)}, u32[]{:S(2)}, u32[]{:S(2)}) collective-permute-start(bf16[128,1152]{1,0:T(8,128)(2,1)S(1)} %get-tuple-element.79), channel_id=1, source_target_pairs={{0,16},{16,0},{32,48},{48,32},{64,80},{80,64},{96,112},{112,96},{1... | collective-permute-start | bytes 884744 | tf_op jit(solution)/shard_map/ppermute | solution.py:35
  179.3 21.2 %collective-permute-start.17 = (bf16[128,1152]{1,0:T(8,128)(2,1)S(1)}, bf16[128,1152]{1,0:T(8,128)(2,1)S(1)}, u32[]{:S(2)}, u32[]{:S(2)}) collective-permute-start(bf16[128,1152]{1,0:T(8,128)(2,1)S(1)} %get-tuple-element.78), channel_id=1, source_target_pairs={{0,112},{16,96},{32,16},{48,0},{64,48},{80,32},{96,80},{112,64},{1... | collective-permute-start | bytes 884744 | tf_op jit(solution)/shard_map/ppermute | solution.py:35
  182.3 18.2 %collective-permute-start.18 = (bf16[128,1152]{1,0:T(8,128)(2,1)S(1)}, bf16[128,1152]{1,0:T(8,128)(2,1)S(1)}, u32[]{:S(2)}, u32[]{:S(2)}) collective-permute-start(bf16[128,1152]{1,0:T(8,128)(2,1)S(1)} %get-tuple-element.77), channel_id=1, source_target_pairs={{0,48},{16,32},{32,80},{48,64},{64,112},{80,96},{96,16},{112,0},{1... | collective-permute-start | bytes 884744 | tf_op jit(solution)/shard_map/ppermute | solution.py:35
  185.5 18.4 %collective-permute-start.19 = (bf16[128,1152]{1,0:T(8,128)(2,1)S(1)}, bf16[128,1152]{1,0:T(8,128)(2,1)S(1)}, u32[]{:S(2)}, u32[]{:S(2)}) collective-permute-start(bf16[128,1152]{1,0:T(8,128)(2,1)S(1)} %get-tuple-element.76), channel_id=1, source_target_pairs={{0,64},{16,80},{32,96},{48,112},{64,0},{80,16},{96,32},{112,48},{1... | collective-permute-start | bytes 884744 | tf_op jit(solution)/shard_map/ppermute | solution.py:35
  186.8 25.7 %collective-permute-start.20 = (bf16[128,1152]{1,0:T(8,128)(2,1)S(1)}, bf16[128,1152]{1,0:T(8,128)(2,1)S(1)}, u32[]{:S(2)}, u32[]{:S(2)}) collective-permute-start(bf16[128,1152]{1,0:T(8,128)(2,1)S(1)} %get-tuple-element.75), channel_id=1, source_target_pairs={{0,80},{16,64},{32,112},{48,96},{64,16},{80,0},{96,48},{112,32},{1... | collective-permute-start | bytes 884744 | tf_op jit(solution)/shard_map/ppermute | solution.py:35
  218.6 21.6 %collective-permute-start.23 = (bf16[128,1152]{1,0:T(8,128)(2,1)}, bf16[128,1152]{1,0:T(8,128)(2,1)S(1)}, u32[]{:S(2)}, u32[]{:S(2)}) collective-permute-start(bf16[128,1152]{1,0:T(8,128)(2,1)} %get-tuple-element.50), channel_id=1, source_target_pairs={{0,16},{16,0},{32,48},{48,32},{64,80},{80,64},{96,112},{112,96},{1... | collective-permute-start | bytes 884744 | tf_op jit(solution)/shard_map/ppermute | solution.py:35
  218.9 22.0 %collective-permute-start.24 = (bf16[128,1152]{1,0:T(8,128)(2,1)}, bf16[128,1152]{1,0:T(8,128)(2,1)S(1)}, u32[]{:S(2)}, u32[]{:S(2)}) collective-permute-start(bf16[128,1152]{1,0:T(8,128)(2,1)} %get-tuple-element.50), channel_id=1, source_target_pairs={{0,48},{16,32},{32,80},{48,64},{64,112},{80,96},{96,16},{112,0},{1... | collective-permute-start | bytes 884744 | tf_op jit(solution)/shard_map/ppermute | solution.py:35
  220.2 21.5 %collective-permute-start.25 = (bf16[128,1152]{1,0:T(8,128)(2,1)}, bf16[128,1152]{1,0:T(8,128)(2,1)S(1)}, u32[]{:S(2)}, u32[]{:S(2)}) collective-permute-start(bf16[128,1152]{1,0:T(8,128)(2,1)} %get-tuple-element.50), channel_id=1, source_target_pairs={{0,112},{16,96},{32,16},{48,0},{64,48},{80,32},{96,80},{112,64},{1... | collective-permute-start | bytes 884744 | tf_op jit(solution)/shard_map/ppermute | solution.py:35
  224.8 17.6 %collective-permute-start.26 = (bf16[128,1152]{1,0:T(8,128)(2,1)}, bf16[128,1152]{1,0:T(8,128)(2,1)S(1)}, u32[]{:S(2)}, u32[]{:S(2)}) collective-permute-start(bf16[128,1152]{1,0:T(8,128)(2,1)} %get-tuple-element.50), channel_id=1, source_target_pairs={{0,64},{16,80},{32,96},{48,112},{64,0},{80,16},{96,32},{112,48},{1... | collective-permute-start | bytes 884744 | tf_op jit(solution)/shard_map/ppermute | solution.py:35
  226.5 18.4 %collective-permute-start.27 = (bf16[128,1152]{1,0:T(8,128)(2,1)}, bf16[128,1152]{1,0:T(8,128)(2,1)S(1)}, u32[]{:S(2)}, u32[]{:S(2)}) collective-permute-start(bf16[128,1152]{1,0:T(8,128)(2,1)} %get-tuple-element.50), channel_id=1, source_target_pairs={{0,80},{16,64},{32,112},{48,96},{64,16},{80,0},{96,48},{112,32},{1... | collective-permute-start | bytes 884744 | tf_op jit(solution)/shard_map/ppermute | solution.py:35
  271.3 15.0 %collective-permute-start.28 = (bf16[128,1152]{1,0:T(8,128)(2,1)S(1)}, bf16[128,1152]{1,0:T(8,128)(2,1)S(1)}, u32[]{:S(2)}, u32[]{:S(2)}) collective-permute-start(bf16[128,1152]{1,0:T(8,128)(2,1)S(1)} %get-tuple-element.67), channel_id=1, source_target_pairs={{0,96},{16,112},{32,0},{48,16},{64,32},{80,48},{96,64},{112,80},{1... | collective-permute-start | bytes 884744 | tf_op jit(solution)/shard_map/ppermute | solution.py:35
  280.5 18.7 %collective-permute-start.30 = (bf16[128,1152]{1,0:T(8,128)(2,1)S(1)}, bf16[128,1152]{1,0:T(8,128)(2,1)S(1)}, u32[]{:S(2)}, u32[]{:S(2)}) collective-permute-start(bf16[128,1152]{1,0:T(8,128)(2,1)S(1)} %get-tuple-element.72), channel_id=1, source_target_pairs={{0,16},{16,0},{32,48},{48,32},{64,80},{80,64},{96,112},{112,96},{1... | collective-permute-start | bytes 884744 | tf_op jit(solution)/shard_map/ppermute | solution.py:35
  282.4 22.6 %collective-permute-start.31 = (bf16[128,1152]{1,0:T(8,128)(2,1)S(1)}, bf16[128,1152]{1,0:T(8,128)(2,1)S(1)}, u32[]{:S(2)}, u32[]{:S(2)}) collective-permute-start(bf16[128,1152]{1,0:T(8,128)(2,1)S(1)} %get-tuple-element.71), channel_id=1, source_target_pairs={{0,112},{16,96},{32,16},{48,0},{64,48},{80,32},{96,80},{112,64},{1... | collective-permute-start | bytes 884744 | tf_op jit(solution)/shard_map/ppermute | solution.py:35
  285.8 19.2 %collective-permute-start.32 = (bf16[128,1152]{1,0:T(8,128)(2,1)S(1)}, bf16[128,1152]{1,0:T(8,128)(2,1)S(1)}, u32[]{:S(2)}, u32[]{:S(2)}) collective-permute-start(bf16[128,1152]{1,0:T(8,128)(2,1)S(1)} %get-tuple-element.70), channel_id=1, source_target_pairs={{0,48},{16,32},{32,80},{48,64},{64,112},{80,96},{96,16},{112,0},{1... | collective-permute-start | bytes 884744 | tf_op jit(solution)/shard_map/ppermute | solution.py:35
  286.3 18.7 %collective-permute-start.33 = (bf16[128,1152]{1,0:T(8,128)(2,1)S(1)}, bf16[128,1152]{1,0:T(8,128)(2,1)S(1)}, u32[]{:S(2)}, u32[]{:S(2)}) collective-permute-start(bf16[128,1152]{1,0:T(8,128)(2,1)S(1)} %get-tuple-element.69), channel_id=1, source_target_pairs={{0,64},{16,80},{32,96},{48,112},{64,0},{80,16},{96,32},{112,48},{1... | collective-permute-start | bytes 884744 | tf_op jit(solution)/shard_map/ppermute | solution.py:35
  287.6 21.2 %collective-permute-start.34 = (bf16[128,1152]{1,0:T(8,128)(2,1)S(1)}, bf16[128,1152]{1,0:T(8,128)(2,1)S(1)}, u32[]{:S(2)}, u32[]{:S(2)}) collective-permute-start(bf16[128,1152]{1,0:T(8,128)(2,1)S(1)} %get-tuple-element.68), channel_id=1, source_target_pairs={{0,80},{16,64},{32,112},{48,96},{64,16},{80,0},{96,48},{112,32},{1... | collective-permute-start | bytes 884744 | tf_op jit(solution)/shard_map/ppermute | solution.py:35
  299.2 37.7 %collective-permute-start.50 = (bf16[4,1152,256]{1,2,0:T(8,128)(2,1)}, bf16[4,1152,256]{1,2,0:T(8,128)(2,1)}, u32[]{:S(2)}, u32[]{:S(2)}) collective-permute-start(bf16[4,1152,256]{1,2,0:T(8,128)(2,1)} %pad_maximum_fusion.1), channel_id=1, source_target_pairs={{0,1},{1,0},{2,3},{3,2},{4,5},{5,4},{6,7},{7,6},{8,9},{9,8},{10,11... | collective-permute-start | bytes 7077896 | tf_op jit(solution)/shard_map/ppermute | solution.py:39
  305.0 23.5 %collective-permute-start.51 = (bf16[4,1152,128]{1,2,0:T(8,128)(2,1)}, bf16[4,1152,128]{1,2,0:T(8,128)(2,1)}, u32[]{:S(2)}, u32[]{:S(2)}) collective-permute-start(bf16[4,1152,128]{1,2,0:T(8,128)(2,1)} %slice.452), channel_id=1, source_target_pairs={{0,1},{1,0},{2,3},{3,2},{4,5},{5,4},{6,7},{7,6},{8,9},{9,8},{10,11... | collective-permute-start | bytes 3538952 | tf_op jit(solution)/shard_map/ppermute | solution.py:39
  316.1 96.1 %collective-permute-start.47 = (bf16[4,1152,128]{1,2,0:T(8,128)(2,1)}, bf16[4,1152,128]{1,2,0:T(8,128)(2,1)}, u32[]{:S(2)}, u32[]{:S(2)}) collective-permute-start(bf16[4,1152,128]{1,2,0:T(8,128)(2,1)} %dynamic-slice_bitcast_fusion.1), channel_id=1, source_target_pairs={{0,1},{1,0},{2,3},{3,2},{4,5},{5,4},{6,7},{7,6},{8,9},{9,8},{10,11... | collective-permute-start | bytes 3538952 | tf_op jit(solution)/shard_map/ppermute | solution.py:39
  325.3 34.2 %collective-permute-start.35 = (bf16[1,128,512]{2,1,0:T(8,128)(2,1)}, bf16[1,128,512]{2,1,0:T(8,128)(2,1)S(1)}, u32[]{:S(2)}, u32[]{:S(2)}) collective-permute-start(bf16[1,128,512]{2,1,0:T(8,128)(2,1)} %get-tuple-element.107), channel_id=1, source_target_pairs={{16,0},{32,16},{48,32},{64,48},{80,64},{96,80},{112,96},{17,1},{33... | collective-permute-start | bytes 393224 | tf_op jit(solution)/shard_map/ppermute | solution.py:30
  326.8 32.8 %collective-permute-start.36 = (bf16[1,128,512]{2,1,0:T(8,128)(2,1)}, bf16[1,128,512]{2,1,0:T(8,128)(2,1)S(1)}, u32[]{:S(2)}, u32[]{:S(2)}) collective-permute-start(bf16[1,128,512]{2,1,0:T(8,128)(2,1)} %get-tuple-element.110), channel_id=1, source_target_pairs={{32,0},{48,16},{64,32},{80,48},{96,64},{112,80},{33,1},{49,17},{65... | collective-permute-start | bytes 393224 | tf_op jit(solution)/shard_map/ppermute | solution.py:30
  328.5 31.1 %collective-permute-start.37 = (bf16[1,128,512]{2,1,0:T(8,128)(2,1)}, bf16[1,128,512]{2,1,0:T(8,128)(2,1)S(1)}, u32[]{:S(2)}, u32[]{:S(2)}) collective-permute-start(bf16[1,128,512]{2,1,0:T(8,128)(2,1)} %get-tuple-element.109), channel_id=1, source_target_pairs={{48,0},{64,16},{80,32},{96,48},{112,64},{49,1},{65,17},{81,33},{97... | collective-permute-start | bytes 393224 | tf_op jit(solution)/shard_map/ppermute | solution.py:30
  332.5 21.0 %all-to-all-start.9 = ((bf16[4,1152,128]{1,2,0:T(8,128)(2,1)}), bf16[4,1152,128]{1,2,0:T(8,128)(2,1)}, u32[]{:S(2)}, u32[]{:S(2)}) async-start(bf16[4,1152,128]{1,2,0:T(8,128)(2,1)} %add_convert_fusion.1), calls=%async_computation.9 | async-start | bytes 2359296 | tf_op jit(solution)/shard_map/all_to_all | solution.py:55
  336.9 22.7 %collective-permute-start.38 = (bf16[1,128,512]{2,1,0:T(8,128)(2,1)}, bf16[1,128,512]{2,1,0:T(8,128)(2,1)S(1)}, u32[]{:S(2)}, u32[]{:S(2)}) collective-permute-start(bf16[1,128,512]{2,1,0:T(8,128)(2,1)} %get-tuple-element.108), channel_id=1, source_target_pairs={{64,0},{80,16},{96,32},{112,48},{65,1},{81,17},{97,33},{113,49},{6... | collective-permute-start | bytes 393224 | tf_op jit(solution)/shard_map/ppermute | solution.py:30
  353.5 33.2 %all-to-all-start.8 = ((bf16[4,1152,256]{1,2,0:T(8,128)(2,1)}), bf16[4,1152,256]{1,2,0:T(8,128)(2,1)}, u32[]{:S(2)}, u32[]{:S(2)}) async-start(bf16[4,1152,256]{1,2,0:T(8,128)(2,1)} %add_convert_fusion), calls=%async_computation.8 | async-start | bytes 4718592 | tf_op jit(solution)/shard_map/all_to_all | solution.py:55
  390.4 21.2 %all-to-all-start.10 = ((bf16[8,144,384]{2,1,0:T(8,128)(2,1)}), bf16[8,144,384]{2,1,0:T(8,128)(2,1)}, u32[]{:S(2)}, u32[]{:S(2)}) async-start(bf16[8,144,384]{2,1,0:T(8,128)(2,1)} %bitcast.81), calls=%async_computation.10 | async-start | bytes 1769472 | tf_op jit(solution)/shard_map/all_to_all | solution.py:55
  411.7 17.3 %collective-permute-start.52 = (bf16[8,144,384]{2,1,0:T(8,128)(2,1)}, bf16[8,144,384]{2,1,0:T(8,128)(2,1)}, u32[]{:S(2)}, u32[]{:S(2)}) collective-permute-start(bf16[8,144,384]{2,1,0:T(8,128)(2,1)} %all-to-all-done.10), channel_id=1, source_target_pairs={{0,2},{2,0},{1,3},{3,1},{4,6},{6,4},{5,7},{7,5},{8,10},{10,8},{9,1... | collective-permute-start | bytes 2654216 | tf_op jit(solution)/shard_map/ppermute | solution.py:39
  414.8 15.9 %all-to-all-start.5 = ((bf16[4,1152,128]{1,2,0:T(8,128)(2,1)}), bf16[4,1152,128]{1,2,0:T(8,128)(2,1)S(1)}, u32[]{:S(2)}, u32[]{:S(2)}) async-start(bf16[4,1152,128]{1,2,0:T(8,128)(2,1)} %fusion.9), calls=%async_computation.5 | async-start | bytes 2359296 | tf_op jit(solution)/shard_map/all_to_all | solution.py:55
  424.4 13.0 %collective-permute-start.46 = (bf16[4,1152,256]{2,1,0:T(8,128)(2,1)}, bf16[4,1152,256]{2,1,0:T(8,128)(2,1)}, u32[]{:S(2)}, u32[]{:S(2)}) collective-permute-start(bf16[4,1152,256]{2,1,0:T(8,128)(2,1)} %dynamic-slice_bitcast_fusion), channel_id=1, source_target_pairs={{0,1},{1,0},{2,3},{3,2},{4,5},{5,4},{6,7},{7,6},{8,9},{9,8},{10,11... | collective-permute-start | bytes 7077896 | tf_op jit(solution)/shard_map/ppermute | solution.py:39
  432.9 41.9 %all-to-all-start.11 = ((bf16[4,8,144,384]{3,2,1,0:T(8,128)(2,1)}), bf16[4,8,144,384]{3,2,1,0:T(8,128)(2,1)S(1)}, u32[]{:S(2)}, u32[]{:S(2)}) async-start(bf16[4,8,144,384]{3,2,1,0:T(8,128)(2,1)} %broadcast_in_dim.89), calls=%async_computation.11 | async-start | bytes 7077888 | tf_op jit(solution)/shard_map/all_to_all | solution.py:55
  474.8 28.4 %all-to-all-start.4 = ((bf16[4,1152,256]{2,1,0:T(8,128)(2,1)}), bf16[4,1152,256]{2,1,0:T(8,128)(2,1)}, u32[]{:S(2)}, u32[]{:S(2)}) async-start(bf16[4,1152,256]{2,1,0:T(8,128)(2,1)} %fusion), calls=%async_computation.4 | async-start | bytes 4718592 | tf_op jit(solution)/shard_map/all_to_all | solution.py:55
  479.4 108.5 %collective-permute-start.53 = (bf16[4,8,144,384]{3,2,1,0:T(8,128)(2,1)S(1)}, bf16[4,8,144,384]{3,2,1,0:T(8,128)(2,1)}, u32[]{:S(2)}, u32[]{:S(2)}) collective-permute-start(bf16[4,8,144,384]{3,2,1,0:T(8,128)(2,1)S(1)} %all-to-all-done.11.mine_ref), channel_id=1, source_target_pairs={{0,1},{1,0},{2,3},{3,2},{4,5},{5,4},{6,7},{7,6},{8,9},{9,8},{10,11... | collective-permute-start | bytes 10616840 | tf_op jit(solution)/shard_map/ppermute | solution.py:39
  509.3 46.2 %all-to-all-start.6 = ((bf16[8,144,384]{2,1,0:T(8,128)(2,1)}), bf16[8,144,384]{2,1,0:T(8,128)(2,1)}, u32[]{:S(2)}, u32[]{:S(2)}) async-start(bf16[8,144,384]{2,1,0:T(8,128)(2,1)} %bitcast.249), calls=%async_computation.6 | async-start | bytes 1769472 | tf_op jit(solution)/shard_map/all_to_all | solution.py:55
  (87 other events, 960.2 us)
